TPU v7x, 256 devices: a whole 4x4x8 slice. The times are simulated.
256 devices in a mesh: pix: 32 (over z, y), ang: 8 (over x, core).
Axes of the slice: x: 4, y: 4, z: 8, core: 2. Of those that a mesh axis runs over, the one named last changes fastest.
Arguments:
- tiles: float32 [32, 8, 512, 4096], P('pix', 'ang'), may hold values from 0.01 to 1
- tile_ray: int32 [32, 8, 512], P('pix', 'ang'), may hold values from 0 to 127, as said below
- tile_pix: int32 [32, 8, 512], P('pix', 'ang'), may hold values from 0 to 15, as said below
- tile_count: int32 [32, 8], P('pix', 'ang'), may hold values from 128 to 512, as said below
- ray_slot: int32 [8, 128], P('ang'), may hold values from 0 to 127, as said below
- image: float32 [32768, 128], P(('pix', 'ang')), may hold values from 0 to 2
- measured: float32 [8, 8192, 128], P('ang', 'pix'), may hold values from -6144 to 6144
Outputs:
- new_image: float32 [32768, 128], P(('pix', 'ang'))
- scaled_resid: float32 [8, 8192, 128], P('ang', 'pix')
Inputs may be any that keep to these rules, and one draw needn't show every extreme that they name: Device (p, a) uses only its first tile_count[p, a] tiles; some device uses all 512. `tile_ray`: the used tiles of the devices of one angle group a together name every ray block of that group. `tile_pix`: the used tiles of the devices of one region p together name every pixel block of that region. `ray_slot`: each row is a permutation; slot s lies on the device with pix index s // 4.
All inputs are finite; a program needn't handle non-finite values.
Results may differ from a plain program's by a relative error of at most 0.0003.
Values sent between devices are 32-bit elements; how exact they have to be, the bound alone decides.
A program may use at most 64 MiB of HBM per device.

v0:
```python
import math

import jax
import jax.numpy as jnp
from jax import lax
from jax.sharding import PartitionSpec as P

BLK = 64
S = 128
SLOTS = 512
PXB_DEV = 2


relax_factor = 0.9


def shards(tiles, tile_ray, tile_pix, tile_count, ray_slot, image, measured):
    slot_table = ray_slot[0]
    ray_total = slot_table.shape[0]
    pixel_blocks_all = PXB_DEV * lax.axis_size("ang")
    matrices_all = tiles[0, 0]
    ray_index = tile_ray[0, 0]
    pixel_index = tile_pix[0, 0]
    used_tiles = tile_count[0, 0]
    block_ids = jnp.arange(ray_total, dtype=jnp.int32)
    slot_index = jnp.sum(
        jnp.where(ray_index[:, None] == block_ids[None, :], slot_table[None, :], 0), axis=1
    )
    region_rows = lax.all_gather(image, "ang", axis=0, tiled=True)
    region_blocks = region_rows.reshape(pixel_blocks_all, BLK, S)
    block_size = math.gcd(32, SLOTS)
    blocks_used = (used_tiles + block_size - 1) // block_size

    def load_block(block_index):
        first_tile = block_index * block_size
        flat = lax.dynamic_slice_in_dim(matrices_all, first_tile, block_size, 0)
        active = (first_tile + jnp.arange(block_size, dtype=jnp.int32) < used_tiles).astype(
            jnp.float32
        )
        matrices = flat.reshape(block_size, BLK, BLK) * active[:, None, None]
        pixel_ids = lax.dynamic_slice_in_dim(pixel_index, first_tile, block_size, 0)
        slot_ids = lax.dynamic_slice_in_dim(slot_index, first_tile, block_size, 0)
        return (matrices, pixel_ids, slot_ids)

    def forward(block_index, state_tuple):
        proj, row_sums, col_sums = state_tuple
        matrices, pixel_ids, slot_ids = load_block(block_index)
        contrib = jnp.einsum(
            "tij,tjs->tis", matrices, region_blocks[pixel_ids], precision=lax.Precision.HIGHEST
        )
        proj = proj.at[slot_ids].add(contrib)
        row_sums = row_sums.at[slot_ids].add(jnp.sum(matrices, axis=2))
        col_sums = col_sums.at[pixel_ids].add(jnp.sum(matrices, axis=1))
        return (proj, row_sums, col_sums)

    start_state = (
        jnp.zeros((ray_total, BLK, S), jnp.float32),
        jnp.zeros((ray_total, BLK), jnp.float32),
        jnp.zeros((pixel_blocks_all, BLK), jnp.float32),
    )
    proj, row_sums, col_sums = lax.fori_loop(0, blocks_used, forward, start_state)
    proj_rows = proj.reshape(ray_total * BLK, S)
    row_totals = row_sums.reshape(ray_total * BLK)
    summed, row_norms = (
        lax.psum_scatter(proj_rows, "pix", scatter_dimension=0, tiled=True),
        lax.psum_scatter(row_totals, "pix", scatter_dimension=0, tiled=True),
    )
    resid_own = (measured[0] - summed) / row_norms[:, None]
    resid_all = lax.all_gather(resid_own, "pix", axis=0, tiled=True)
    resid_blocks = resid_all.reshape(ray_total, BLK, S)

    def backward(block_index, back_sums):
        matrices, pixel_ids, slot_ids = load_block(block_index)
        contrib = jnp.einsum(
            "tij,tis->tjs", matrices, resid_blocks[slot_ids], precision=lax.Precision.HIGHEST
        )
        return back_sums.at[pixel_ids].add(contrib)

    back_sums = lax.fori_loop(
        0, blocks_used, backward, jnp.zeros((pixel_blocks_all, BLK, S), jnp.float32)
    )
    back_own, column_norms = (
        lax.psum_scatter(
            back_sums.reshape(pixel_blocks_all * BLK, S), "ang", scatter_dimension=0, tiled=True
        ),
        lax.psum_scatter(
            col_sums.reshape(pixel_blocks_all * BLK), "ang", scatter_dimension=0, tiled=True
        ),
    )
    new_image = image + relax_factor * back_own / column_norms[:, None]
    return (new_image, resid_own[None])


def solution(mesh):
    in_specs = (
        P("pix", "ang", None, None),
        P("pix", "ang", None),
        P("pix", "ang", None),
        P("pix", "ang"),
        P("ang", None),
        P(("pix", "ang"), None),
        P("ang", "pix", None),
    )
    out_specs = (P(("pix", "ang"), None), P("ang", "pix", None))
    return jax.shard_map(shards, mesh=mesh, in_specs=in_specs, out_specs=out_specs, check_vma=False)
```

profile of v0, /device:TPU:1, one launch (start us, length us, event | category | flops | bytes accessed | tf_op | source)
XLA Modules:
  0.0 751.1 jit_solution(7539857111754736717)
XLA Ops:
  7.9 17.5 %all_gather.6 = f32[1024,128]{1,0:T(8,128)} all-gather(f32[128,128]{1,0:T(8,128)} %param.16), channel_id=1, replica_groups=mesh['pix'=32,'ang'=8] {'ang'}, dimensions={0}, use_global_device_ids=true | all-gather | bytes 589824 | tf_op jit(solution)/shard_map/all_gather | solution.py:29
  28.8 119.6 %while.24 = (s32[]{:T(128)}, f32[128,64,128]{2,1,0:T(8,128)}, f32[128,64]{1,0:T(8,128)S(1)}, f32[16,64]{1,0:T(8,128)S(1)}, s32[]{:T(128)}, /*index=5*/s32[512]{0...) while((s32[]{:T(128)}, f32[128,64,128]{2,1,0:T(8,128)}, ...), condition=%wide.region_7.8_spmd, body=%wide.region_1.7_spmd.sunk | while | flops 202114336 | bytes 10557123 | solution.py:61
  36.0 4.8 scatter_fusion
  47.9 4.8 scatter_fusion
  59.9 4.8 scatter_fusion
  71.8 4.8 scatter_fusion
  83.8 4.8 scatter_fusion
  95.7 4.8 scatter_fusion
  107.7 4.8 scatter_fusion
  119.6 4.8 scatter_fusion
  131.6 4.8 scatter_fusion
  143.6 4.8 scatter_fusion
  150.4 179.7 %all-reduce = f32[8192]{0:T(1024)S(1)} all-reduce(f32[8192]{0:T(1024)S(1)} %reshape.45), channel_id=3, replica_groups=mesh['pix'=32,'ang'=8] {'pix'}, use_global_device_ids=true, to_apply=%region_9.10.clone | all-reduce | flops 8192 | bytes 65536
  330.2 106.6 %reduce-scatter.3.cloned.1.call-done = f32[256,128]{1,0:T(8,128)} async-done(((f32[8192,128]{1,0:T(8,128)}), f32[256,128]{1,0:T(8,128)}) %reduce-scatter.3.cloned.1.call-update) | async-done | bytes 131088 | tf_op jit(solution)/shard_map/reduce_scatter | solution.py:65
  438.6 84.3 %all-gather.2.cloned.1.call-done = f32[8192,128]{1,0:T(8,128)} async-done(((f32[256,128]{1,0:T(8,128)}), f32[8192,128]{1,0:T(8,128)}) %all-gather.2.cloned.1.call-update) | async-done | bytes 4194320 | tf_op jit(solution)/shard_map/all_gather | solution.py:69
  523.7 118.0 %while.25 = (s32[]{:T(128)}, f32[16,64,128]{2,1,0:T(8,128)}, s32[]{:T(128)}, s32[512]{0:T(512)S(1)}, f32[512,4096]{1,0:T(8,128)}, /*index=5*/s32[]{:T(128)}, s32...) while((s32[]{:T(128)}, f32[16,64,128]{2,1,0:T(8,128)}, ...), condition=%wide.region_12.13_spmd, body=%wide.region_10.12_spmd.sunk | while | flops 201721120 | bytes 9966899 | solution.py:79
  526.0 2.8 gather_fusion.1
  530.8 4.8 scatter_fusion.3
  537.8 2.8 gather_fusion.1
  542.5 4.8 scatter_fusion.3
  554.3 4.8 scatter_fusion.3
  561.4 2.8 gather_fusion.1
  566.2 4.8 scatter_fusion.3
  573.2 2.8 gather_fusion.1
  578.0 4.8 scatter_fusion.3
  589.8 4.8 scatter_fusion.3
  601.6 4.8 scatter_fusion.3
  613.4 4.8 scatter_fusion.3
  625.2 4.8 scatter_fusion.3
  636.9 4.8 scatter_fusion.3
  643.1 80.1 %all-reduce.1 = f32[1024]{0:T(1024)S(1)} all-reduce(f32[1024]{0:T(1024)S(1)} %reshape.48), channel_id=5, replica_groups=mesh['pix'=32,'ang'=8] {'ang'}, use_global_device_ids=true, to_apply=%region_14.15.clone | all-reduce | flops 1024 | bytes 8192
  723.3 19.7 %reduce-scatter.5.cloned.1.call-done = f32[128,128]{1,0:T(8,128)} async-done(((f32[1024,128]{1,0:T(8,128)}), f32[128,128]{1,0:T(8,128)}) %reduce-scatter.5.cloned.1.call-update) | async-done | bytes 65552 | tf_op jit(solution)/shard_map/reduce_scatter | solution.py:83
  (195 shorter events, 139.5 us)
Async XLA Ops:
  7.2 21.6 %copy-start.2 = (s32[1,1,512]{2,1,0:T(1,128)S(1)}, s32[1,1,512]{2,1,0:T(1,128)}, u32[]{:S(2)}) copy-start(s32[1,1,512]{2,1,0:T(1,128)} %param.13) | copy-start | bytes 6148
  7.2 429.6 %reduce-scatter.3.cloned.1.call-start = ((), (), s32[]{:S(2)}) async-start(), calls=%async_computation.2 | async-start | bytes 4325376 | tf_op jit(solution)/shard_map/reduce_scatter | solution.py:65
  148.4 0.7 copy-start.4
  148.4 288.4 %copy-start.1 = (f32[1,256,128]{2,1,0:T(8,128)S(1)}, f32[1,256,128]{2,1,0:T(8,128)}, u32[]{:S(2)}) copy-start(f32[1,256,128]{2,1,0:T(8,128)} %param.17) | copy-start | bytes 393220
  148.4 374.4 %all-gather.2.cloned.1.call-start = ((), (), s32[]{:S(2)}) async-start(), calls=%async_computation.3 | async-start | bytes 4325376 | tf_op jit(solution)/shard_map/all_gather | solution.py:69
  438.5 304.5 %reduce-scatter.5.cloned.1.call-start = ((), (), s32[]{:S(2)}) async-start(), calls=%async_computation.4 | async-start | bytes 589824 | tf_op jit(solution)/shard_map/reduce_scatter | solution.py:83
  523.7 118.0 %copy-start.3 = (u32[256]{0:T(256)S(1)}, u32[256]{0:T(256)}, u32[]{:S(2)}) copy-start(u32[256]{0:T(256)} %constant.68) | copy-start | bytes 3076
  523.7 219.3 %copy-start = (f32[128,128]{1,0:T(8,128)S(1)}, f32[128,128]{1,0:T(8,128)}, u32[]{:S(2)}) copy-start(f32[128,128]{1,0:T(8,128)} %param.16) | copy-start | bytes 196612
Sparse Core Ops, SparseCore 0:
  148.5 288.2 reduce-scatter.2
  440.3 82.5 all-gather.1
  641.9 101.0 reduce-scatter.4
where the time goes:
time: 762 us; the launch traced here: 751 us
  blocking collectives  277 us (36%)
  waiting for transfers between devices  211 us (28%)
  other arithmetic  134 us (18%)
  local copies, waits for them, and re-layouts  79.8 us (10%)
  matrix products  32.4 us (4%)
  between operations  15.8 us (2%)
    unnamed x2, blocking collectives  260 us
    reduce_scatter x1, waiting for transfers between devices, shards(): lax.psum_scatter(proj_rows, 'pix', scatter_dimension=0, tiled=True)  107 us
    all_gather x1, waiting for transfers between devices, shards(): resid_all = lax.all_gather(resid_own, 'pix', axis=0, tiled=True)  84.3 us
    scatter-add x10, other arithmetic, backward(): return back_sums.at[pixel_ids].add(contrib)  47.9 us
    scatter-add x10, other arithmetic, forward(): proj = proj.at[slot_ids].add(contrib)  47.8 us
    gather x10, local copies, waits for them, and re-layouts, backward(): resid_blocks[slot_ids]  28.1 us
    dynamic_slice x20, local copies, waits for them, and re-layouts, load_block(): flat = lax.dynamic_slice_in_dim(matrices_all, first_tile, block_size, 0)  21.6 us
    reduce_scatter x1, waiting for transfers between devices, shards(): lax.psum_scatter(back_sums.reshape(pixel_blocks_all * BLK, S), 'ang', sca...  19.7 us
  transfers between devices with their start and end apart: 3, of which 3 were waited for; matrix products, arithmetic and copies ran while one was open for 0% of the time, Pallas kernels for 0%

commit v1 on v0

v1 whole, which is shorter than its diff:
```python
import functools

import jax
import jax.numpy as jnp
from jax import lax
from jax.experimental import pallas as pl
from jax.experimental.pallas import tpu as pltpu
from jax.sharding import PartitionSpec as P

MESH = pl.DeviceIdType.MESH
BLK, S, SLOTS, RB, QB = 64, 128, 512, 128, 16
RELAX = 0.9
NZ, NY, NA = 8, 4, 8
GRP = 4
NPOS = SLOTS + QB * (GRP - 1)
NPOS_PAD = 640
OWN = 256
CH = OWN + 8
VM = pl.BlockSpec(memory_space=pltpu.VMEM)
SM = pl.BlockSpec(memory_space=pltpu.SMEM)
MIB = 1024 * 1024


def vmem(*shape, dtype=jnp.float32):
    return pltpu.VMEM(shape, dtype)


def gather_kernel(img_ref, out_ref, send_sem, recv_sem):
    me = lax.axis_index("ang")
    pix = lax.axis_index("pix")
    barrier = pltpu.get_barrier_semaphore()
    for d in range(1, NA):
        pl.semaphore_signal(barrier, inc=1, device_id=(pix, lax.rem(me + d, NA)), device_id_type=MESH)
    pl.semaphore_wait(barrier, NA - 1)
    rows = pl.ds(pl.multiple_of(me * 128, 128), 128)
    copies = []
    for d in (4, 3, 5, 2, 6, 1, 7):
        copy = pltpu.make_async_remote_copy(
            src_ref=img_ref,
            dst_ref=out_ref.at[rows],
            send_sem=send_sem.at[d - 1],
            recv_sem=recv_sem.at[d - 1],
            device_id=(pix, lax.rem(me + d, NA)),
            device_id_type=MESH,
        )
        copy.start()
        copies.append(copy)
    out_ref[rows, :] = img_ref[...]
    for copy in copies:
        copy.wait()


def gather_image(image):
    return pl.pallas_call(
        gather_kernel,
        out_shape=jax.ShapeDtypeStruct((NA * 128, S), jnp.float32),
        in_specs=[VM],
        out_specs=VM,
        scratch_shapes=[pltpu.SemaphoreType.DMA((NA - 1,)), pltpu.SemaphoreType.DMA((NA - 1,))],
        compiler_params=pltpu.CompilerParams(collective_id=0, has_side_effects=True),
        name="gather_image",
    )(image)


def tile_rows(tiles_ref, code):
    t = lax.shift_right_logical(code, 7) & (SLOTS - 1)
    start = lax.shift_right_logical(t, 3) * 256 + (t & 7)
    used = lax.shift_right_logical(code, 20).astype(jnp.float32)
    return tiles_ref[pl.ds(start, 32, stride=8), :] * used


def forward_kernel(code_ref, count_ref, tiles_ref, img_ref, p_ref, col_ref, w_ref, rowacc, colacc):
    lane_low = lax.broadcasted_iota(jnp.int32, (32, 128), 1) < BLK

    def weights(q, _):
        x = img_ref[pl.ds(pl.multiple_of(q * BLK, BLK), BLK), :]
        hi = x.astype(jnp.bfloat16)
        lo = (x - hi.astype(jnp.float32)).astype(jnp.bfloat16)
        w_ref[q] = jnp.concatenate([hi, hi, lo, lo], axis=0)
        return _

    lax.fori_loop(0, QB, weights, 0)
    rowacc[...] = jnp.zeros_like(rowacc)
    colacc[...] = jnp.zeros_like(colacc)

    def clear(o, _):
        p_ref[o] = jnp.zeros((CH, S), jnp.float32)
        return _

    lax.fori_loop(0, NZ * NY, clear, 0)

    def group(g, _):
        codes = [code_ref[g * GRP + i] for i in range(GRP)]
        q = lax.shift_right_logical(codes[0], 16) & (QB - 1)
        tiles = [tile_rows(tiles_ref, c) for c in codes]
        parts = []
        for m in tiles:
            hi = m.astype(jnp.bfloat16).astype(jnp.float32)
            lo = m - hi
            parts.append(jnp.where(lane_low, hi, pltpu.roll(lo, BLK, 1)))
            parts.append(jnp.where(lane_low, pltpu.roll(hi, BLK, 1), lo))
        x = jnp.concatenate(parts, axis=0).astype(jnp.bfloat16)
        out = jnp.dot(jnp.concatenate([x, x], axis=1), w_ref[q], preferred_element_type=jnp.float32)
        for i, (c, m) in enumerate(zip(codes, tiles)):
            slot = c & (RB - 1)
            rows = pl.ds(pl.multiple_of((slot & 3) * BLK, BLK), BLK)
            owner = lax.shift_right_logical(slot, 2)
            p_ref[owner, rows, :] += out[BLK * i : BLK * (i + 1)]
            rowacc[slot] += m
        colacc[q] += (tiles[0] + tiles[1]) + (tiles[2] + tiles[3])
        return _

    lax.fori_loop(0, count_ref[0], group, 0)

    pick = lax.broadcasted_iota(jnp.int32, (8, 128), 0) == (lax.broadcasted_iota(jnp.int32, (8, 128), 1) // BLK)
    pick = pick.astype(jnp.float32).astype(jnp.bfloat16)

    def row_sums(o, _):
        x = rowacc[pl.ds(o * 4, 4)].reshape(128, 128)
        hi = x.astype(jnp.bfloat16)
        lo = (x - hi.astype(jnp.float32)).astype(jnp.bfloat16)
        dims = (((1,), (1,)), ((), ()))
        sums = lax.dot_general(pick, hi, dims, preferred_element_type=jnp.float32)
        sums += lax.dot_general(pick, lo, dims, preferred_element_type=jnp.float32)
        p_ref[o, OWN:CH, :] = sums
        return _

    lax.fori_loop(0, NZ * NY, row_sums, 0)
    low = lax.broadcasted_iota(jnp.int32, (1, 128), 1) < BLK
    for o in range(NA):
        a = jnp.sum(colacc[2 * o], axis=0, keepdims=True)
        b = jnp.sum(colacc[2 * o + 1], axis=0, keepdims=True)
        a = a + pltpu.roll(a, BLK, 1)
        b = b + pltpu.roll(b, BLK, 1)
        col_ref[o] = jnp.broadcast_to(jnp.where(low, a, b), (8, 128))


def forward(code, count, tiles, img):
    return pl.pallas_call(
        forward_kernel,
        out_shape=(
            jax.ShapeDtypeStruct((NZ * NY, CH, S), jnp.float32),
            jax.ShapeDtypeStruct((NA, 8, 128), jnp.float32),
        ),
        in_specs=[SM, SM, VM, VM],
        out_specs=(VM, VM),
        scratch_shapes=[
            vmem(QB, 4 * BLK, S, dtype=jnp.bfloat16),
            vmem(RB, 32, 128),
            vmem(QB, 32, 128),
        ],
        compiler_params=pltpu.CompilerParams(vmem_limit_bytes=40 * MIB),
        name="forward_tiles",
    )(code, count, tiles, img)


def ring_steps(n, sign):
    return ((sign, n // 2), (-sign, n // 2 - 1))


class Task:
    def __init__(self, key, link, rows, needs):
        self.key, self.link, self.rows, self.needs = key, link, rows, needs


def schedule(tasks, latency, rate):
    by_key = {t.key: t for t in tasks}
    follow = {t.key: [] for t in tasks}
    for t in tasks:
        for k in t.needs:
            follow[k].append(t.key)
    tail = {}

    def tail_of(k):
        if k not in tail:
            t = by_key[k]
            tail[k] = t.rows / rate + latency + max([tail_of(f) for f in follow[k]], default=0.0)
        return tail[k]

    left, done, free, order = list(tasks), {}, {}, []
    while left:
        best = None
        for t in left:
            if all(k in done for k in t.needs):
                at = max([done[k] for k in t.needs], default=0.0)
                start = max(at, free.get(t.link, 0.0))
                rank = (start, -tail_of(t.key))
                if best is None or rank < best[0]:
                    best = (rank, t)
        (start, _), t = best
        free[t.link] = start + t.rows / rate
        done[t.key] = start + t.rows / rate + latency
        order.append((start, t.key))
        left.remove(t)
    return [k for _, k in sorted(order, key=lambda e: e[0])]


RATE = 95.0
LATENCY = 1.5

SUM_A = (0, 104)
SUM_B = (104, 264)
ALL_A = (0, 104)
ALL_B = (104, 256)


def halves(span):
    lo, hi = span
    mid = lo + ((hi - lo) // 2 + 7) // 8 * 8
    return ((lo, mid), (mid, hi))


def sign_of(i):
    return 1 if i % 2 == 0 else -1


def sum_tasks():
    tasks = []

    def ring(stage, n, axis, piece, sign, rows, local_needs):
        for chain, (d, steps) in enumerate(ring_steps(n, sign)):
            for s in range(1, steps + 1):
                off = (d * (steps - s + 1)) % n
                needs = [(stage, piece, chain, s - 1)] if s > 1 else []
                tasks.append(Task((stage, piece, chain, s), (axis, d), rows, needs + local_needs(off)))

    def last(stage, n, piece):
        return [(stage, piece, 0, n // 2), (stage, piece, 1, n // 2 - 1)]

    for yo in range(NY):
        ring("a1", NZ, "z", yo, sign_of(yo), SUM_A[1] - SUM_A[0], lambda off: [])
    for h, (lo, hi) in enumerate(halves(SUM_A)):
        ring("a2", NY, "y", h, sign_of(h), hi - lo, lambda off: last("a1", NZ, off))
    for zo in range(NZ):
        ring("b1", NY, "y", zo, sign_of(zo), SUM_B[1] - SUM_B[0], lambda off: [])
    for h, (lo, hi) in enumerate(halves(SUM_B)):
        ring("b2", NZ, "z", h, sign_of(h), hi - lo, lambda off: last("b1", NY, off))
    return tasks


def all_tasks():
    tasks = []

    def ring(stage, n, axis, piece, sign, rows, first_needs):
        for chain, (d, steps) in enumerate(ring_steps(n, sign)):
            for s in range(1, steps + 1):
                needs = [(stage, piece, chain, s - 1)] if s > 1 else first_needs
                tasks.append(Task((stage, piece, chain, s), (axis, d), rows, needs))

    def arrives(stage, n, piece, sign, off):
        for chain, (d, steps) in enumerate(ring_steps(n, sign)):
            for s in range(1, steps + 1):
                if (-d * s) % n == off:
                    return (stage, piece, chain, s)

    for h, (lo, hi) in enumerate(halves(ALL_A)):
        ring("c1", NY, "y", h, sign_of(h), hi - lo, [])
    for yo in range(NY):
        needs = [arrives("c1", NY, h, sign_of(h), yo) for h in range(2)] if yo else []
        ring("c2", NZ, "z", yo, sign_of(yo), ALL_A[1] - ALL_A[0], needs)
    for h, (lo, hi) in enumerate(halves(ALL_B)):
        ring("d1", NZ, "z", h, sign_of(h), hi - lo, [])
    for zo in range(NZ):
        needs = [arrives("d1", NZ, h, sign_of(h), zo) for h in range(2)] if zo else []
        ring("d2", NY, "y", zo, sign_of(zo), ALL_B[1] - ALL_B[0], needs)
    return tasks


AHEAD = 3


def exchange_kernel(p_ref, meas_ref, resid_ref, all_ref, ra1, ra2, rb1, rb2, own, send_sem, recv_sem):
    pix, ang = lax.axis_index("pix"), lax.axis_index("ang")
    z, y = pix // NY, lax.rem(pix, NY)

    def at(zo, yo):
        return lax.rem(z + zo % NZ, NZ) * NY + lax.rem(y + yo % NY, NY)

    def device(link):
        axis, d = link
        return (at(d, 0) if axis == "z" else at(0, d), ang)

    barrier = pltpu.get_barrier_semaphore()
    for link in (("z", 1), ("z", -1), ("y", 1), ("y", -1)):
        pl.semaphore_signal(barrier, inc=1, device_id=device(link), device_id_type=MESH)
    pl.semaphore_wait(barrier, 4)

    tasks = sum_tasks() + all_tasks()
    number = {t.key: i for i, t in enumerate(tasks)}
    by_key = {t.key: t for t in tasks}
    sums = schedule(sum_tasks(), LATENCY, RATE)
    alls = schedule(all_tasks(), LATENCY, RATE)

    a_rows, b_rows = pl.ds(SUM_A[0], SUM_A[1] - SUM_A[0]), pl.ds(SUM_B[0], SUM_B[1] - SUM_B[0])
    slot_of = {}
    for stage, ref in (("a1", ra1), ("a2", ra2), ("b1", rb1), ("b2", rb2)):
        keys = [t.key for t in tasks if t.key[0] == stage]
        for i, k in enumerate(keys):
            slot_of[k] = ref.at[i, pl.ds(0, by_key[k].rows)]

    def chain_of(n, piece, chain):
        return ring_steps(n, sign_of(piece))[chain]

    def origin(key):
        stage, piece, chain, s = key
        if stage in ("c1", "d1"):
            n = NY if stage == "c1" else NZ
            d, _ = chain_of(n, piece, chain)
            off = -d * (s - 1)
            lo, hi = halves(ALL_A if stage == "c1" else ALL_B)[piece]
            return (at(0, off) if stage == "c1" else at(off, 0)), pl.ds(lo, hi - lo)
        n = NZ if stage == "c2" else NY
        d, _ = chain_of(n, piece, chain)
        off = -d * (s - 1)
        lo, hi = ALL_A if stage == "c2" else ALL_B
        return (at(off, piece) if stage == "c2" else at(piece, off)), pl.ds(lo, hi - lo)

    def source(key):
        stage, piece, chain, s = key
        if stage in ("c1", "c2", "d1", "d2"):
            owner, rows = origin(key)
            ref = all_ref.at[owner, rows]
            return ref, ref
        dst = slot_of[key]
        if s > 1:
            return slot_of[(stage, piece, chain, s - 1)], dst
        return local(key), dst

    def local(key):
        stage, piece, chain, s = key
        if stage in ("a1", "b1"):
            n = NZ if stage == "a1" else NY
            d, steps = chain_of(n, piece, chain)
            off = d * (steps - s + 1)
            return p_ref.at[at(off, piece), a_rows] if stage == "a1" else p_ref.at[at(piece, off), b_rows]
        n = NY if stage == "a2" else NZ
        d, steps = chain_of(n, piece, chain)
        off = (d * (steps - s + 1)) % n
        span = SUM_A if stage == "a2" else SUM_B
        lo, hi = halves(span)[piece]
        first = ("a1" if stage == "a2" else "b1", off, 0, n_first(stage) // 2)
        return slot_of[first].at[pl.ds(lo - span[0], hi - lo)]

    def n_first(stage):
        return NZ if stage == "a2" else NY

    copies = {}

    def copy_of(key):
        if key not in copies:
            src, dst = source(key)
            i = number[key]
            copies[key] = pltpu.make_async_remote_copy(
                src_ref=src,
                dst_ref=dst,
                send_sem=send_sem.at[i],
                recv_sem=recv_sem.at[i],
                device_id=device(by_key[key].link),
                device_id_type=MESH,
            )
        return copies[key]

    received, sent, waited, finished = set(), {}, set(), set()

    def receive(key):
        if key not in received:
            received.add(key)
            copy_of(key).wait_recv()

    def finish(stage, off):
        if (stage, off) in finished:
            return
        finished.add((stage, off))
        n = NZ if stage == "a1" else NY
        one, two = (stage, off, 0, n // 2), (stage, off, 1, n // 2 - 1)
        receive(one)
        receive(two)
        mine = p_ref.at[at(0, off), a_rows] if stage == "a1" else p_ref.at[at(off, 0), b_rows]
        slot_of[one][...] = slot_of[one][...] + slot_of[two][...] + mine[...]

    def issue(key):
        stage, piece, chain, s = key
        task = by_key[key]
        queue = sent.setdefault(task.link, [])
        if len(queue) >= AHEAD:
            old = queue[-AHEAD]
            if old not in waited:
                waited.add(old)
                copy_of(old).wait_send()
        for k in task.needs:
            if stage in ("a2", "b2") and k[0] in ("a1", "b1"):
                finish(k[0], k[1])
            else:
                receive(k)
        if s > 1 and stage in ("a1", "a2", "b1", "b2"):
            ref = slot_of[(stage, piece, chain, s - 1)]
            ref[...] = ref[...] + local(key)[...]
        copy_of(key).start()
        queue.append(key)

    for key in sums:
        issue(key)
    for stage, span, n, n1 in (("a2", SUM_A, NY, NZ), ("b2", SUM_B, NZ, NY)):
        first = "a1" if stage == "a2" else "b1"
        finish(first, 0)
        for h, (lo, hi) in enumerate(halves(span)):
            one, two = (stage, h, 0, n // 2), (stage, h, 1, n // 2 - 1)
            receive(one)
            receive(two)
            mine = slot_of[(first, 0, 0, n1 // 2)].at[pl.ds(lo - span[0], hi - lo)]
            own[lo:hi, :] = slot_of[one][...] + slot_of[two][...] + mine[...]

    norms = [jnp.broadcast_to(own[OWN + h : OWN + h + 1, :], (128, 128)).T for h in range(2)]
    for b in range(4):
        for h in range(2):
            natural = pl.ds(b * BLK + h, 32, stride=2)
            mine = slice(b * BLK + 32 * h, b * BLK + 32 * h + 32)
            value = (meas_ref[natural, :] - own[mine, :]) / norms[h][32 * b : 32 * b + 32]
            resid_ref[natural, :] = value
            all_ref[at(0, 0), mine, :] = value

    for key in alls:
        issue(key)
    for t in tasks:
        receive(t.key)
    for t in tasks:
        if t.key not in waited:
            copy_of(t.key).wait_send()


def exchange(p, measured):
    tasks = sum_tasks() + all_tasks()
    count = {}
    for t in tasks:
        count[t.key[0]] = count.get(t.key[0], 0) + 1
    most = {k: max(t.rows for t in tasks if t.key[0] == k) for k in count}
    return pl.pallas_call(
        exchange_kernel,
        out_shape=(
            jax.ShapeDtypeStruct((OWN, S), jnp.float32),
            jax.ShapeDtypeStruct((NZ * NY, OWN, S), jnp.float32),
        ),
        in_specs=[VM, VM],
        out_specs=(VM, VM),
        scratch_shapes=[vmem(count[k], most[k], S) for k in ("a1", "a2", "b1", "b2")]
        + [
            vmem(CH, S),
            pltpu.SemaphoreType.DMA((len(tasks),)),
            pltpu.SemaphoreType.DMA((len(tasks),)),
        ],
        compiler_params=pltpu.CompilerParams(
            collective_id=1, has_side_effects=True, vmem_limit_bytes=32 * MIB
        ),
        name="sum_and_spread",
    )(p, measured)


def backward_kernel(code_ref, count_ref, tiles_ref, all_ref, col_ref, b_ref, hi_ref, lo_ref):
    def split(o, _):
        x = all_ref[o]
        hi = x.astype(jnp.bfloat16)
        rows = pl.ds(pl.multiple_of(o * OWN, OWN), OWN)
        hi_ref[rows, :] = hi
        lo_ref[rows, :] = (x - hi.astype(jnp.float32)).astype(jnp.bfloat16)
        return _

    lax.fori_loop(0, NZ * NY, split, 0)
    for o in range(NA):
        b_ref[o, 0:128, :] = jnp.zeros((128, S), jnp.float32)
        b_ref[o, 128:136, :] = col_ref[o]

    def group(g, _):
        codes = [code_ref[g * GRP + i] for i in range(GRP)]
        q = lax.shift_right_logical(codes[0], 16) & (QB - 1)
        x = jnp.concatenate([tile_rows(tiles_ref, c) for c in codes], axis=0).T
        hi = x.astype(jnp.bfloat16)
        lo = (x - hi.astype(jnp.float32)).astype(jnp.bfloat16)
        starts = [(c & (RB - 1)) * BLK for c in codes]

        def rays(ref):
            return [
                ref[pl.ds(pl.multiple_of(start + 32 * h, 32), 32), :] for h in range(2) for start in starts
            ]

        r_hi, r_lo = rays(hi_ref), rays(lo_ref)
        left = jnp.concatenate([hi[:BLK], hi[BLK:], lo[:BLK], lo[BLK:], hi[:BLK], hi[BLK:]], axis=1)
        right = jnp.concatenate(r_hi + r_hi + r_lo, axis=0)
        out = jnp.dot(left, right, preferred_element_type=jnp.float32)
        rows = pl.ds(pl.multiple_of((q & 1) * BLK, BLK), BLK)
        b_ref[lax.shift_right_logical(q, 1), rows, :] += out
        return _

    lax.fori_loop(0, count_ref[0], group, 0)


def backward(code, count, tiles, everyone, col):
    return pl.pallas_call(
        backward_kernel,
        out_shape=jax.ShapeDtypeStruct((NA, 136, S), jnp.float32),
        in_specs=[SM, SM, VM, VM, VM],
        out_specs=VM,
        scratch_shapes=[
            vmem(RB * BLK, S, dtype=jnp.bfloat16),
            vmem(RB * BLK, S, dtype=jnp.bfloat16),
        ],
        compiler_params=pltpu.CompilerParams(vmem_limit_bytes=40 * MIB),
        name="backward_tiles",
    )(code, count, tiles, everyone, col)


def update_kernel(b_ref, img_ref, out_ref, got, send_sem, recv_sem):
    me = lax.axis_index("ang")
    pix = lax.axis_index("pix")
    barrier = pltpu.get_barrier_semaphore()
    for d in range(1, NA):
        pl.semaphore_signal(barrier, inc=1, device_id=(pix, lax.rem(me + d, NA)), device_id_type=MESH)
    pl.semaphore_wait(barrier, NA - 1)
    copies = []
    for d in (4, 3, 5, 2, 6, 1, 7):
        to = lax.rem(me + d, NA)
        copy = pltpu.make_async_remote_copy(
            src_ref=b_ref.at[to],
            dst_ref=got.at[d - 1],
            send_sem=send_sem.at[d - 1],
            recv_sem=recv_sem.at[d - 1],
            device_id=(pix, to),
            device_id_type=MESH,
        )
        copy.start()
        copies.append(copy)
    for copy in copies:
        copy.wait()
    total = b_ref[me]
    for d in range(NA - 1):
        total = total + got[d]
    norm = jnp.broadcast_to(total[128:129], (128, 128)).T
    out_ref[...] = img_ref[...] + RELAX * (total[:128] / norm)


def update(b, image):
    return pl.pallas_call(
        update_kernel,
        out_shape=jax.ShapeDtypeStruct((128, S), jnp.float32),
        in_specs=[VM, VM],
        out_specs=VM,
        scratch_shapes=[
            vmem(NA - 1, 136, S),
            pltpu.SemaphoreType.DMA((NA - 1,)),
            pltpu.SemaphoreType.DMA((NA - 1,)),
        ],
        compiler_params=pltpu.CompilerParams(collective_id=2, has_side_effects=True),
        name="sum_and_update",
    )(b, image)


def sort_tiles(tile_ray, tile_pix, tile_count, slot_table):
    t = jnp.arange(SLOTS, dtype=jnp.int32)
    used = t < tile_count
    slot = jnp.sum(
        jnp.where(tile_ray[:, None] == jnp.arange(RB, dtype=jnp.int32)[None, :], slot_table[None, :], 0), axis=1
    )
    q = jnp.where(used, tile_pix, QB)
    before = jnp.sum(((q[None, :] == q[:, None]) & (t[None, :] < t[:, None])).astype(jnp.int32), axis=1)
    blocks = jnp.arange(QB, dtype=jnp.int32)
    counts = jnp.sum((q[None, :] == blocks[:, None]).astype(jnp.int32), axis=1)
    whole = (counts + GRP - 1) // GRP * GRP
    first = jnp.sum(jnp.where(blocks[None, :] < q[:, None], whole[None, :], 0), axis=1)
    place = jnp.where(used, first + before, -1)
    code = (1 << 20) | (q << 16) | (t << 7) | slot
    places = jnp.arange(NPOS_PAD, dtype=jnp.int32)
    listed = jnp.sum(jnp.where(place[None, :] == places[:, None], code[None, :], 0), axis=1)
    return listed, jnp.sum(whole, keepdims=True) // GRP


def shards(tiles, tile_ray, tile_pix, tile_count, ray_slot, image, measured):
    code, count = sort_tiles(tile_ray[0, 0], tile_pix[0, 0], tile_count[0, 0], ray_slot[0])
    rows = tiles[0, 0].reshape(SLOTS // 8, 8, 32, 128).transpose(0, 2, 1, 3).reshape(SLOTS * 32, 128)
    img = gather_image(image)
    p, col = forward(code, count, rows, img)
    resid, everyone = exchange(p, measured[0])
    b = backward(code, count, rows, everyone, col)
    new_image = update(b, image)
    return (new_image, resid[None])


def solution(mesh):
    in_specs = (
        P("pix", "ang", None, None),
        P("pix", "ang", None),
        P("pix", "ang", None),
        P("pix", "ang"),
        P("ang", None),
        P(("pix", "ang"), None),
        P("ang", "pix", None),
    )
    out_specs = (P(("pix", "ang"), None), P("ang", "pix", None))
    return jax.shard_map(shards, mesh=mesh, in_specs=in_specs, out_specs=out_specs, check_vma=False)
```

time: 762 us -> 172 us (0.23)
  the two profiles are of different devices: /device:TPU:1 before, /device:TPU:136 now
where the time goes in v1:
time: 172 us
  Pallas kernels  157 us (91%)
  local copies, waits for them, and re-layouts  7.34 us (4%)
  between operations  3.97 us (2%)
  other arithmetic  2.94 us (2%)
    pallas_call x1, Pallas kernels, exchange(): pl.pallas_call(exchange_kernel, out_shape=(jax.ShapeDtypeStruct((OWN, S),...  59.3 us
    pallas_call x1, Pallas kernels, forward(): pl.pallas_call(forward_kernel, out_shape=(jax.ShapeDtypeStruct((NZ * NY,...  39.5 us
    pallas_call x1, Pallas kernels, backward(): pl.pallas_call(backward_kernel, out_shape=jax.ShapeDtypeStruct((NA, 136,...  33.9 us
    pallas_call x1, Pallas kernels, gather_image(): pl.pallas_call(gather_kernel, out_shape=jax.ShapeDtypeStruct((NA * 128, S...  12.5 us
    pallas_call x1, Pallas kernels, update(): pl.pallas_call(update_kernel, out_shape=jax.ShapeDtypeStruct((128, S), jn...  12.1 us
    unnamed x12, local copies, waits for them, and re-layouts  7.34 us

profile of v1, /device:TPU:136, one launch (start us, length us, event | category | flops | bytes accessed | tf_op | source)
XLA Modules:
  0.0 171.6 jit_solution(15352271802108140878)
XLA Ops:
  1.3 0.9 select_reduce_fusion.1
  2.2 0.7 or_or_fusion
  2.9 0.1 convert_reduce_fusion.1
  3.0 0.6 fusion.3
  6.3 0.1 select_reduce_fusion.2
  6.4 0.2 convert_reduce_fusion
  6.6 0.2 select_reduce_fusion.code_ref
  6.8 12.5 %gather_image.1.img_ref = f32[1024,128]{1,0:T(8,128)} custom-call(f32[128,128]{1,0:T(8,128)} %img_ref.3), custom_call_target="tpu_custom_call" | custom-call | tf_op jit(solution)/shard_map/gather_image/pallas_call | solution.py:54
  19.4 0.0 copy-start
  19.4 3.4 %copy-done = f32[1,1,512,4096]{3,2,1,0:T(8,128)S(1)} copy-done((f32[1,1,512,4096]{3,2,1,0:T(8,128)S(1)}, f32[1,1,512,4096]{3,2,1,0:T(8,128)}, u32[]{:S(2)}) %copy-start) | copy-done | bytes 8388632
  22.8 0.0 copy-start.3
  22.8 1.0 copy-done.3
  23.8 0.0 copy-start.4
  23.8 0.0 copy-start.1
  23.8 39.5 %forward_tiles.1 = (f32[32,264,128]{2,1,0:T(8,128)S(1)}, f32[8,8,128]{2,1,0:T(8,128)S(1)}) custom-call(s32[640]{0:T(1024)S(1)} %select_reduce_fusion.code_ref, s32[1]{0:T(128)S(6)} %select_n.54.count_ref, f32[16384,128]{1,0:T(8,128)S(1)} %bitcast.14, f32[1024,128]{1,0:T(8,128)S(1)} %copy-done.3), custom_call_target="tpu_custom_call" | custom-call | tf_op jit(solution)/shard_map/forward_tiles/pallas_call | solution.py:139
  63.4 0.0 copy-done.4
  63.4 59.3 %sum_and_spread.1 = (f32[256,128]{1,0:T(8,128)S(1)}, f32[32,256,128]{2,1,0:T(8,128)S(1)}) custom-call(f32[32,264,128]{2,1,0:T(8,128)S(1)} %get-tuple-element.6.p_ref, f32[256,128]{1,0:T(8,128)S(1)} %bitcast.16), custom_call_target="tpu_custom_call" | custom-call | tf_op jit(solution)/shard_map/sum_and_spread/pallas_call | solution.py:437
  122.7 0.0 copy-done.1
  122.7 33.9 %backward_tiles.1.b_ref = f32[8,136,128]{2,1,0:T(8,128)S(1)} custom-call(s32[640]{0:T(1024)S(1)} %select_reduce_fusion.code_ref, s32[1]{0:T(128)S(6)} %select_n.54.count_ref, f32[16384,128]{1,0:T(8,128)S(1)} %bitcast.15, f32[32,256,128]{2,1,0:T(8,128)S(1)} %get-tuple-element.7.all_ref, f32[8,8,128]{2,1,0:T(8,128)S(1)} %get-tuple-element.8.col_ref), custom_call_target="tpu_custom_call" | custom-call | tf_op jit(solution)/shard_map/backward_tiles/pallas_call | solution.py:497
  156.6 0.0 copy-start.2
  156.6 0.8 copy-done.2
  157.4 12.1 %sum_and_update.1 = f32[128,128]{1,0:T(8,128)} custom-call(f32[8,136,128]{2,1,0:T(8,128)} %copy-done.2, f32[128,128]{1,0:T(8,128)} %img_ref.3), custom_call_target="tpu_custom_call" | custom-call | tf_op jit(solution)/shard_map/sum_and_update/pallas_call | solution.py:541
  169.5 1.5 copy.12
  171.0 0.7 copy.13
  (1 shorter events, 0.0 us)
Async XLA Ops:
  19.4 3.4 %copy-start = (f32[1,1,512,4096]{3,2,1,0:T(8,128)S(1)}, f32[1,1,512,4096]{3,2,1,0:T(8,128)}, u32[]{:S(2)}) copy-start(f32[1,1,512,4096]{3,2,1,0:T(8,128)} %param.7) | copy-start | bytes 25165828
  22.8 1.0 copy-start.3
  23.8 39.6 %copy-start.4 = (f32[1,256,128]{2,1,0:T(8,128)S(1)}, f32[1,256,128]{2,1,0:T(8,128)}, u32[]{:S(2)}) copy-start(f32[1,256,128]{2,1,0:T(8,128)} %param.13) | copy-start | bytes 393220
  23.8 98.9 %copy-start.1 = (f32[1,1,512,4096]{3,2,1,0:T(8,128)S(1)}, f32[1,1,512,4096]{3,2,1,0:T(8,128)}, u32[]{:S(2)}) copy-start(f32[1,1,512,4096]{3,2,1,0:T(8,128)} %param.7) | copy-start | bytes 25165828
  156.6 0.8 copy-start.2

commit v2 on v1

--- a/solution.py
+++ b/solution.py
@@ -10,7 +10,7 @@
 MESH = pl.DeviceIdType.MESH
 BLK, S, SLOTS, RB, QB = 64, 128, 512, 128, 16
 RELAX = 0.9
-NZ, NY, NA = 8, 4, 8
+NZ, NY, NX, NA = 8, 4, 4, 8
 GRP = 4
 NPOS = SLOTS + QB * (GRP - 1)
 NPOS_PAD = 640
@@ -21,45 +21,135 @@
 MIB = 1024 * 1024
 
 
+def cost(us):
+    return pl.CostEstimate(flops=int(us * 1.15e9), bytes_accessed=0, transcendentals=0)
+
+
 def vmem(*shape, dtype=jnp.float32):
     return pltpu.VMEM(shape, dtype)
 
 
-def gather_kernel(img_ref, out_ref, send_sem, recv_sem):
-    me = lax.axis_index("ang")
-    pix = lax.axis_index("pix")
-    barrier = pltpu.get_barrier_semaphore()
-    for d in range(1, NA):
-        pl.semaphore_signal(barrier, inc=1, device_id=(pix, lax.rem(me + d, NA)), device_id_type=MESH)
-    pl.semaphore_wait(barrier, NA - 1)
-    rows = pl.ds(pl.multiple_of(me * 128, 128), 128)
-    copies = []
-    for d in (4, 3, 5, 2, 6, 1, 7):
+def split_bf16(x):
+    hi = x.astype(jnp.bfloat16)
+    return hi, (x - hi.astype(jnp.float32)).astype(jnp.bfloat16)
+
+
+def sign_of(i):
+    return 1 if i % 2 == 0 else -1
+
+
+class Ang:
+    def __init__(self):
+        self.pix, me = lax.axis_index("pix"), lax.axis_index("ang")
+        self.me, self.x, self.core = me, me // 2, lax.rem(me, 2)
+
+    def index(self, dx):
+        return lax.rem(self.x + dx % NX, NX) * 2 + self.core
+
+    def twin(self, dx=0):
+        return lax.rem(self.x + dx % NX, NX) * 2 + (1 - self.core)
+
+    def device(self, to):
+        return (self.pix, self.twin() if to == "twin" else self.index(to))
+
+    def meet(self):
+        barrier = pltpu.get_barrier_semaphore()
+        for to in ("twin", 1, -1):
+            pl.semaphore_signal(barrier, inc=1, device_id=self.device(to), device_id_type=MESH)
+        pl.semaphore_wait(barrier, 3)
+
+
+def sort_tiles(ray, pix, used_tiles, table):
+    f32 = jnp.float32
+    both = jnp.broadcast_to((pix * RB + ray).astype(f32), (128, SLOTS)).T.astype(jnp.int32)
+    lane = lax.broadcasted_iota(jnp.int32, (SLOTS, 128), 1)
+    t = lax.broadcasted_iota(jnp.int32, (SLOTS, 128), 0)
+    q = lax.shift_right_logical(both, 7)
+    mine = jnp.where((q == lane) & (t < used_tiles), 1.0, 0.0).astype(f32)
+    slot = jnp.sum(jnp.where((both & (RB - 1)) == lane, table.astype(f32), 0.0), axis=1, keepdims=True)
+    earlier = lax.broadcasted_iota(jnp.int32, (SLOTS, SLOTS), 1) < lax.broadcasted_iota(jnp.int32, (SLOTS, SLOTS), 0)
+    earlier = jnp.where(earlier, 1.0, 0.0).astype(jnp.bfloat16)
+    before = jnp.dot(earlier, mine.astype(jnp.bfloat16), preferred_element_type=f32)
+    counts = jnp.sum(mine, axis=0, keepdims=True).astype(jnp.int32)
+    groups = lax.shift_right_logical(counts + (GRP - 1), 2).astype(f32)
+    left_of = lax.broadcasted_iota(jnp.int32, (128, 128), 0) < lax.broadcasted_iota(jnp.int32, (128, 128), 1)
+    left_of = jnp.where(left_of, 1.0, 0.0).astype(jnp.bfloat16)
+    first = jnp.dot(jnp.broadcast_to(groups, (8, 128)).astype(jnp.bfloat16), left_of, preferred_element_type=f32)
+    place = jnp.sum(mine * (before + GRP * first[:1]), axis=1, keepdims=True)
+    place = jnp.where(t < used_tiles, place, -1.0)
+    code = ((1 << 20) + q * (1 << 16) + t * RB).astype(f32) + slot
+    parts = []
+    for c in range(NPOS_PAD // 128):
+        at = (lax.broadcasted_iota(jnp.int32, (1, 128), 1) + c * 128).astype(f32)
+        part = jnp.sum(jnp.where(place == at, code, 0.0), axis=0, keepdims=True)
+        parts.append(jnp.where(at == NPOS_PAD - 1, jnp.sum(groups, axis=1, keepdims=True), part))
+    return jnp.concatenate(parts, axis=1).astype(jnp.int32)
+
+
+def gather_kernel(
+    count_ref, ray_ref, pix_ref, table_ref, img_ref, out_ref, code_ref, send_sem, recv_sem
+):
+    here = Ang()
+    here.meet()
+    number = iter(range(13))
+
+    def send(to, dx, half, src=None):
+        lo, size = (0, 128) if half is None else (64 * half, 64)
+        rows = out_ref.at[pl.ds(pl.multiple_of(here.index(dx) * 128 + lo, 64), size)]
+        i = next(number)
         copy = pltpu.make_async_remote_copy(
-            src_ref=img_ref,
-            dst_ref=out_ref.at[rows],
-            send_sem=send_sem.at[d - 1],
-            recv_sem=recv_sem.at[d - 1],
-            device_id=(pix, lax.rem(me + d, NA)),
+            src_ref=rows if src is None else src.at[pl.ds(lo, size)],
+            dst_ref=rows,
+            send_sem=send_sem.at[i],
+            recv_sem=recv_sem.at[i],
+            device_id=here.device(to),
             device_id_type=MESH,
         )
         copy.start()
-        copies.append(copy)
-    out_ref[rows, :] = img_ref[...]
-    for copy in copies:
-        copy.wait()
-
-
-def gather_image(image):
+        return copy
+
+    far = [send(sign_of(h), 0, h, img_ref) for h in range(2)]
+    near = [send(-sign_of(h), 0, h, img_ref) for h in range(2)]
+    across = [send("twin", 0, None, img_ref)]
+    out_ref[pl.ds(pl.multiple_of(here.me * 128, 128), 128), :] = img_ref[...]
+    code_ref[...] = sort_tiles(ray_ref[...], pix_ref[...], count_ref[0, 0], table_ref[...])
+    second = []
+    for h in range(2):
+        far[h].wait_recv()
+        second.append(send(sign_of(h), -sign_of(h), h))
+    for h in range(2):
+        across.append(send("twin", -sign_of(h), h))
+    for h in range(2):
+        near[h].wait_recv()
+        across.append(send("twin", sign_of(h), h))
+    for h in range(2):
+        second[h].wait_recv()
+        across.append(send("twin", 2, h))
+    for copy in across:
+        copy.wait_recv()
+    for copy in far + near + second + across:
+        copy.wait_send()
+
+
+def gather_image(count, ray, pix, table, image):
     return pl.pallas_call(
         gather_kernel,
-        out_shape=jax.ShapeDtypeStruct((NA * 128, S), jnp.float32),
-        in_specs=[VM],
-        out_specs=VM,
-        scratch_shapes=[pltpu.SemaphoreType.DMA((NA - 1,)), pltpu.SemaphoreType.DMA((NA - 1,))],
-        compiler_params=pltpu.CompilerParams(collective_id=0, has_side_effects=True),
+        out_shape=(
+            jax.ShapeDtypeStruct((NA * 128, S), jnp.float32),
+            jax.ShapeDtypeStruct((1, NPOS_PAD), jnp.int32),
+        ),
+        in_specs=[SM, VM, VM, VM, VM],
+        out_specs=(VM, VM),
+        scratch_shapes=[
+            pltpu.SemaphoreType.DMA((13,)),
+            pltpu.SemaphoreType.DMA((13,)),
+        ],
+        compiler_params=pltpu.CompilerParams(
+            collective_id=0, has_side_effects=True, vmem_limit_bytes=24 * MIB
+        ),
+        cost_estimate=cost(8),
         name="gather_image",
-    )(image)
+    )(count, ray, pix, table, image)
 
 
 def tile_rows(tiles_ref, code):
@@ -69,17 +159,19 @@
     return tiles_ref[pl.ds(start, 32, stride=8), :] * used
 
 
-def forward_kernel(code_ref, count_ref, tiles_ref, img_ref, p_ref, col_ref, w_ref, rowacc, colacc):
-    lane_low = lax.broadcasted_iota(jnp.int32, (32, 128), 1) < BLK
+FWD = 12
+
+
+def forward_kernel(code_ref, tiles_ref, img_ref, p_ref, col_ref, w_ref, rowacc, colacc):
+    zero = jnp.zeros((BLK, S), jnp.bfloat16)
 
     def weights(q, _):
-        x = img_ref[pl.ds(pl.multiple_of(q * BLK, BLK), BLK), :]
-        hi = x.astype(jnp.bfloat16)
-        lo = (x - hi.astype(jnp.float32)).astype(jnp.bfloat16)
-        w_ref[q] = jnp.concatenate([hi, hi, lo, lo], axis=0)
+        hi, lo = split_bf16(img_ref[pl.ds(pl.multiple_of(q * BLK, BLK), BLK), :])
+        both = [jnp.concatenate([jnp.concatenate([x, zero], 1), jnp.concatenate([zero, x], 1)], 0) for x in (hi, lo)]
+        w_ref[q] = jnp.concatenate([both[0], both[0], both[1]], axis=0)
         return _
 
-    lax.fori_loop(0, QB, weights, 0)
+    lax.fori_loop(0, QB, weights, 0, unroll=4)
     rowacc[...] = jnp.zeros_like(rowacc)
     colacc[...] = jnp.zeros_like(colacc)
 
@@ -87,45 +179,57 @@
         p_ref[o] = jnp.zeros((CH, S), jnp.float32)
         return _
 
-    lax.fori_loop(0, NZ * NY, clear, 0)
-
-    def group(g, _):
-        codes = [code_ref[g * GRP + i] for i in range(GRP)]
-        q = lax.shift_right_logical(codes[0], 16) & (QB - 1)
-        tiles = [tile_rows(tiles_ref, c) for c in codes]
-        parts = []
-        for m in tiles:
-            hi = m.astype(jnp.bfloat16).astype(jnp.float32)
-            lo = m - hi
-            parts.append(jnp.where(lane_low, hi, pltpu.roll(lo, BLK, 1)))
-            parts.append(jnp.where(lane_low, pltpu.roll(hi, BLK, 1), lo))
-        x = jnp.concatenate(parts, axis=0).astype(jnp.bfloat16)
-        out = jnp.dot(jnp.concatenate([x, x], axis=1), w_ref[q], preferred_element_type=jnp.float32)
-        for i, (c, m) in enumerate(zip(codes, tiles)):
-            slot = c & (RB - 1)
-            rows = pl.ds(pl.multiple_of((slot & 3) * BLK, BLK), BLK)
-            owner = lax.shift_right_logical(slot, 2)
-            p_ref[owner, rows, :] += out[BLK * i : BLK * (i + 1)]
-            rowacc[slot] += m
-        colacc[q] += (tiles[0] + tiles[1]) + (tiles[2] + tiles[3])
+    lax.fori_loop(0, NZ * NY, clear, 0, unroll=4)
+
+    def place(slot):
+        rows = pl.ds(pl.multiple_of((slot & 3) * BLK, BLK), BLK)
+        return lax.shift_right_logical(slot, 2), rows, slice(None)
+
+    def read(slot):
+        return p_ref[place(slot)]
+
+    def write(slot, value):
+        p_ref[place(slot)] = value
+
+    def read_rows(slot):
+        return rowacc[slot]
+
+    def write_rows(slot, value):
+        rowacc[slot] = value
+
+    def step(b, _):
+        for i in range(FWD):
+            codes = [code_ref[0, (b * FWD + i) * GRP + j] for j in range(GRP)]
+            q = lax.shift_right_logical(codes[0], 16) & (QB - 1)
+            slots = [c & (RB - 1) for c in codes]
+            tiles = [tile_rows(tiles_ref, c) for c in codes]
+            hi, lo = split_bf16(jnp.concatenate(tiles, axis=0))
+            out = jnp.dot(jnp.concatenate([hi, lo, hi], axis=1), w_ref[q], preferred_element_type=jnp.float32)
+            terms = [
+                jnp.concatenate([out[32 * j : 32 * j + 32, h * S : h * S + S] for h in range(2)], axis=0)
+                for j in range(GRP)
+            ]
+            for k, v in zip(slots, tiles):
+                rowacc[k] += v
+            colacc[q] += (tiles[0] + tiles[1]) + (tiles[2] + tiles[3])
+            for k, v in zip(slots, terms):
+                write(k, read(k) + v)
         return _
 
-    lax.fori_loop(0, count_ref[0], group, 0)
+    lax.fori_loop(0, (code_ref[0, NPOS_PAD - 1] + FWD - 1) // FWD, step, 0)
 
     pick = lax.broadcasted_iota(jnp.int32, (8, 128), 0) == (lax.broadcasted_iota(jnp.int32, (8, 128), 1) // BLK)
     pick = pick.astype(jnp.float32).astype(jnp.bfloat16)
 
     def row_sums(o, _):
-        x = rowacc[pl.ds(o * 4, 4)].reshape(128, 128)
-        hi = x.astype(jnp.bfloat16)
-        lo = (x - hi.astype(jnp.float32)).astype(jnp.bfloat16)
+        hi, lo = split_bf16(rowacc[pl.ds(o * 4, 4)].reshape(128, 128))
         dims = (((1,), (1,)), ((), ()))
         sums = lax.dot_general(pick, hi, dims, preferred_element_type=jnp.float32)
         sums += lax.dot_general(pick, lo, dims, preferred_element_type=jnp.float32)
         p_ref[o, OWN:CH, :] = sums
         return _
 
-    lax.fori_loop(0, NZ * NY, row_sums, 0)
+    lax.fori_loop(0, NZ * NY, row_sums, 0, unroll=16)
     low = lax.broadcasted_iota(jnp.int32, (1, 128), 1) < BLK
     for o in range(NA):
         a = jnp.sum(colacc[2 * o], axis=0, keepdims=True)
@@ -135,23 +239,24 @@
         col_ref[o] = jnp.broadcast_to(jnp.where(low, a, b), (8, 128))
 
 
-def forward(code, count, tiles, img):
+def forward(code, tiles, img):
     return pl.pallas_call(
         forward_kernel,
         out_shape=(
             jax.ShapeDtypeStruct((NZ * NY, CH, S), jnp.float32),
             jax.ShapeDtypeStruct((NA, 8, 128), jnp.float32),
         ),
-        in_specs=[SM, SM, VM, VM],
+        in_specs=[SM, VM, VM],
         out_specs=(VM, VM),
         scratch_shapes=[
-            vmem(QB, 4 * BLK, S, dtype=jnp.bfloat16),
+            vmem(QB, 6 * BLK, 2 * S, dtype=jnp.bfloat16),
             vmem(RB, 32, 128),
             vmem(QB, 32, 128),
         ],
-        compiler_params=pltpu.CompilerParams(vmem_limit_bytes=40 * MIB),
+        compiler_params=pltpu.CompilerParams(vmem_limit_bytes=32 * MIB),
+        cost_estimate=cost(13),
         name="forward_tiles",
-    )(code, count, tiles, img)
+    )(code, tiles, img)
 
 
 def ring_steps(n, sign):
@@ -208,10 +313,6 @@
     lo, hi = span
     mid = lo + ((hi - lo) // 2 + 7) // 8 * 8
     return ((lo, mid), (mid, hi))
-
-
-def sign_of(i):
-    return 1 if i % 2 == 0 else -1
 
 
 def sum_tasks():
@@ -449,138 +550,159 @@
             pltpu.SemaphoreType.DMA((len(tasks),)),
         ],
         compiler_params=pltpu.CompilerParams(
-            collective_id=1, has_side_effects=True, vmem_limit_bytes=32 * MIB
+            collective_id=1, has_side_effects=True, vmem_limit_bytes=24 * MIB
         ),
+        cost_estimate=cost(50),
         name="sum_and_spread",
     )(p, measured)
 
 
-def backward_kernel(code_ref, count_ref, tiles_ref, all_ref, col_ref, b_ref, hi_ref, lo_ref):
+BWD = 12
+
+
+def backward_kernel(code_ref, tiles_ref, all_ref, col_ref, own_ref, b_ref, resid_ref, hi_ref, lo_ref):
+    resid_ref[...] = own_ref[...]
+
     def split(o, _):
-        x = all_ref[o]
-        hi = x.astype(jnp.bfloat16)
         rows = pl.ds(pl.multiple_of(o * OWN, OWN), OWN)
-        hi_ref[rows, :] = hi
-        lo_ref[rows, :] = (x - hi.astype(jnp.float32)).astype(jnp.bfloat16)
+        hi_ref[rows, :], lo_ref[rows, :] = split_bf16(all_ref[o])
         return _
 
-    lax.fori_loop(0, NZ * NY, split, 0)
+    lax.fori_loop(0, NZ * NY, split, 0, unroll=2)
     for o in range(NA):
         b_ref[o, 0:128, :] = jnp.zeros((128, S), jnp.float32)
         b_ref[o, 128:136, :] = col_ref[o]
 
-    def group(g, _):
-        codes = [code_ref[g * GRP + i] for i in range(GRP)]
-        q = lax.shift_right_logical(codes[0], 16) & (QB - 1)
-        x = jnp.concatenate([tile_rows(tiles_ref, c) for c in codes], axis=0).T
-        hi = x.astype(jnp.bfloat16)
-        lo = (x - hi.astype(jnp.float32)).astype(jnp.bfloat16)
-        starts = [(c & (RB - 1)) * BLK for c in codes]
-
-        def rays(ref):
-            return [
-                ref[pl.ds(pl.multiple_of(start + 32 * h, 32), 32), :] for h in range(2) for start in starts
-            ]
-
-        r_hi, r_lo = rays(hi_ref), rays(lo_ref)
-        left = jnp.concatenate([hi[:BLK], hi[BLK:], lo[:BLK], lo[BLK:], hi[:BLK], hi[BLK:]], axis=1)
-        right = jnp.concatenate(r_hi + r_hi + r_lo, axis=0)
-        out = jnp.dot(left, right, preferred_element_type=jnp.float32)
-        rows = pl.ds(pl.multiple_of((q & 1) * BLK, BLK), BLK)
-        b_ref[lax.shift_right_logical(q, 1), rows, :] += out
+    def step(b, _):
+        for i in range(BWD):
+            codes = [code_ref[0, (b * BWD + i) * GRP + j] for j in range(GRP)]
+            q = lax.shift_right_logical(codes[0], 16) & (QB - 1)
+            hi, lo = split_bf16(jnp.concatenate([tile_rows(tiles_ref, c) for c in codes], axis=0).T)
+            starts = [(c & (RB - 1)) * BLK for c in codes]
+
+            def rays(ref):
+                return [
+                    ref[pl.ds(pl.multiple_of(start + 32 * h, 32), 32), :] for h in range(2) for start in starts
+                ]
+
+            r_hi, r_lo = rays(hi_ref), rays(lo_ref)
+            left = jnp.concatenate([hi[:BLK], hi[BLK:], lo[:BLK], lo[BLK:], hi[:BLK], hi[BLK:]], axis=1)
+            right = jnp.concatenate(r_hi + r_hi + r_lo, axis=0)
+            out = jnp.dot(left, right, preferred_element_type=jnp.float32)
+            rows = pl.ds(pl.multiple_of((q & 1) * BLK, BLK), BLK)
+            b_ref[lax.shift_right_logical(q, 1), rows, :] += out
         return _
 
-    lax.fori_loop(0, count_ref[0], group, 0)
-
-
-def backward(code, count, tiles, everyone, col):
+    lax.fori_loop(0, (code_ref[0, NPOS_PAD - 1] + BWD - 1) // BWD, step, 0)
+
+
+def backward(code, tiles, everyone, col, own):
     return pl.pallas_call(
         backward_kernel,
-        out_shape=jax.ShapeDtypeStruct((NA, 136, S), jnp.float32),
-        in_specs=[SM, SM, VM, VM, VM],
-        out_specs=VM,
+        out_shape=(
+            jax.ShapeDtypeStruct((NA, 136, S), jnp.float32),
+            jax.ShapeDtypeStruct((OWN, S), jnp.float32),
+        ),
+        in_specs=[SM, VM, VM, VM, VM],
+        out_specs=(VM, VM),
         scratch_shapes=[
             vmem(RB * BLK, S, dtype=jnp.bfloat16),
             vmem(RB * BLK, S, dtype=jnp.bfloat16),
         ],
-        compiler_params=pltpu.CompilerParams(vmem_limit_bytes=40 * MIB),
+        compiler_params=pltpu.CompilerParams(vmem_limit_bytes=32 * MIB),
+        cost_estimate=cost(10),
         name="backward_tiles",
-    )(code, count, tiles, everyone, col)
-
-
-def update_kernel(b_ref, img_ref, out_ref, got, send_sem, recv_sem):
-    me = lax.axis_index("ang")
-    pix = lax.axis_index("pix")
-    barrier = pltpu.get_barrier_semaphore()
-    for d in range(1, NA):
-        pl.semaphore_signal(barrier, inc=1, device_id=(pix, lax.rem(me + d, NA)), device_id_type=MESH)
-    pl.semaphore_wait(barrier, NA - 1)
-    copies = []
-    for d in (4, 3, 5, 2, 6, 1, 7):
-        to = lax.rem(me + d, NA)
+    )(code, tiles, everyone, col, own)
+
+
+UPD = ((0, 72), (72, 136))
+
+
+def update_kernel(b_ref, out_ref, sib, far_buf, near_buf, second_buf, send_sem, recv_sem):
+    here = Ang()
+    here.meet()
+    number = iter(range(10))
+
+    def send(to, src, dst):
+        i = next(number)
         copy = pltpu.make_async_remote_copy(
-            src_ref=b_ref.at[to],
-            dst_ref=got.at[d - 1],
-            send_sem=send_sem.at[d - 1],
-            recv_sem=recv_sem.at[d - 1],
-            device_id=(pix, to),
+            src_ref=src,
+            dst_ref=dst,
+            send_sem=send_sem.at[i],
+            recv_sem=recv_sem.at[i],
+            device_id=here.device(to),
             device_id_type=MESH,
         )
         copy.start()
-        copies.append(copy)
-    for copy in copies:
-        copy.wait()
-    total = b_ref[me]
-    for d in range(NA - 1):
-        total = total + got[d]
+        return copy
+
+    across = {dx: send("twin", b_ref.at[here.twin(dx)], sib.at[dx]) for dx in (2, 1, 3, 0)}
+
+    def arrive(dx):
+        across[dx].wait_recv()
+        sib[dx] = sib[dx] + b_ref[here.index(dx)]
+
+    def rows(h):
+        return pl.ds(UPD[h][0], UPD[h][1] - UPD[h][0])
+
+    def part(buf, h):
+        return buf.at[h, pl.ds(0, UPD[h][1] - UPD[h][0])]
+
+    arrive(2)
+    far = [send(sign_of(h), sib.at[2, rows(h)], part(far_buf, h)) for h in range(2)]
+    arrive(1)
+    arrive(3)
+    near = [send(-sign_of(h), sib.at[-sign_of(h) % NX, rows(h)], part(near_buf, h)) for h in range(2)]
+    arrive(0)
+    second = []
+    for h in range(2):
+        far[h].wait_recv()
+        part(far_buf, h)[...] = part(far_buf, h)[...] + sib[sign_of(h) % NX, rows(h), :]
+        second.append(send(sign_of(h), part(far_buf, h), part(second_buf, h)))
+    totals = []
+    for h in range(2):
+        near[h].wait_recv()
+        totals.append(sib[0, rows(h), :] + part(near_buf, h)[...])
+    for h in range(2):
+        second[h].wait_recv()
+        totals[h] = totals[h] + part(second_buf, h)[...]
+    total = jnp.concatenate(totals, axis=0)
     norm = jnp.broadcast_to(total[128:129], (128, 128)).T
-    out_ref[...] = img_ref[...] + RELAX * (total[:128] / norm)
-
-
-def update(b, image):
+    out_ref[...] = RELAX * total[:128] / norm
+    for copy in [*across.values(), *far, *near, *second]:
+        copy.wait_send()
+
+
+def update(b):
+    size = UPD[0][1]
     return pl.pallas_call(
         update_kernel,
         out_shape=jax.ShapeDtypeStruct((128, S), jnp.float32),
-        in_specs=[VM, VM],
+        in_specs=[VM],
         out_specs=VM,
         scratch_shapes=[
-            vmem(NA - 1, 136, S),
-            pltpu.SemaphoreType.DMA((NA - 1,)),
-            pltpu.SemaphoreType.DMA((NA - 1,)),
+            vmem(NX, 136, S),
+            vmem(2, size, S),
+            vmem(2, size, S),
+            vmem(2, size, S),
+            pltpu.SemaphoreType.DMA((10,)),
+            pltpu.SemaphoreType.DMA((10,)),
         ],
-        compiler_params=pltpu.CompilerParams(collective_id=2, has_side_effects=True),
-        name="sum_and_update",
-    )(b, image)
-
-
-def sort_tiles(tile_ray, tile_pix, tile_count, slot_table):
-    t = jnp.arange(SLOTS, dtype=jnp.int32)
-    used = t < tile_count
-    slot = jnp.sum(
-        jnp.where(tile_ray[:, None] == jnp.arange(RB, dtype=jnp.int32)[None, :], slot_table[None, :], 0), axis=1
-    )
-    q = jnp.where(used, tile_pix, QB)
-    before = jnp.sum(((q[None, :] == q[:, None]) & (t[None, :] < t[:, None])).astype(jnp.int32), axis=1)
-    blocks = jnp.arange(QB, dtype=jnp.int32)
-    counts = jnp.sum((q[None, :] == blocks[:, None]).astype(jnp.int32), axis=1)
-    whole = (counts + GRP - 1) // GRP * GRP
-    first = jnp.sum(jnp.where(blocks[None, :] < q[:, None], whole[None, :], 0), axis=1)
-    place = jnp.where(used, first + before, -1)
-    code = (1 << 20) | (q << 16) | (t << 7) | slot
-    places = jnp.arange(NPOS_PAD, dtype=jnp.int32)
-    listed = jnp.sum(jnp.where(place[None, :] == places[:, None], code[None, :], 0), axis=1)
-    return listed, jnp.sum(whole, keepdims=True) // GRP
+        compiler_params=pltpu.CompilerParams(
+            collective_id=2, has_side_effects=True, vmem_limit_bytes=24 * MIB
+        ),
+        cost_estimate=cost(7),
+        name="sum_over_angles",
+    )(b)
 
 
 def shards(tiles, tile_ray, tile_pix, tile_count, ray_slot, image, measured):
-    code, count = sort_tiles(tile_ray[0, 0], tile_pix[0, 0], tile_count[0, 0], ray_slot[0])
     rows = tiles[0, 0].reshape(SLOTS // 8, 8, 32, 128).transpose(0, 2, 1, 3).reshape(SLOTS * 32, 128)
-    img = gather_image(image)
-    p, col = forward(code, count, rows, img)
-    resid, everyone = exchange(p, measured[0])
-    b = backward(code, count, rows, everyone, col)
-    new_image = update(b, image)
-    return (new_image, resid[None])
+    img, code = gather_image(tile_count, tile_ray[0], tile_pix[0], ray_slot, image)
+    p, col = forward(code, rows, img)
+    own, everyone = exchange(p, measured[0])
+    b, resid = backward(code, rows, everyone, col, own)
+    return (image + update(b), resid[None])
 
 
 def solution(mesh):

time: 172 us -> 107 us (0.62)
  the two profiles are of different devices: /device:TPU:136 before, /device:TPU:1 now
where the time goes in v2:
time: 107 us; the launch traced here: 106 us
  Pallas kernels  102 us (95%)
  local copies, waits for them, and re-layouts  2.87 us (3%)
  between operations  1.35 us (1%)
    pallas_call x1, Pallas kernels, exchange(): pl.pallas_call(exchange_kernel, out_shape=(jax.ShapeDtypeStruct((OWN, S),...  58.7 us
    pallas_call x1, Pallas kernels, update(): pl.pallas_call(update_kernel, out_shape=jax.ShapeDtypeStruct((128, S), jn...  14.1 us
    pallas_call x1, Pallas kernels, gather_image(): pl.pallas_call(gather_kernel, out_shape=(jax.ShapeDtypeStruct((NA * 128,...  11.1 us
    pallas_call x1, Pallas kernels, forward(): pl.pallas_call(forward_kernel, out_shape=(jax.ShapeDtypeStruct((NZ * NY,...  9.64 us
    pallas_call x1, Pallas kernels, backward(): pl.pallas_call(backward_kernel, out_shape=(jax.ShapeDtypeStruct((NA, 136,...  8.06 us
    unnamed x14, local copies, waits for them, and re-layouts  2.87 us

profile of v2, /device:TPU:1, one launch (start us, length us, event | category | flops | bytes accessed | tf_op | source)
XLA Modules:
  0.0 106.5 jit_solution(17922418372136340879)
XLA Ops:
  1.3 0.0 copy-start
  1.3 0.8 copy-done
  2.1 0.0 copy-start.4
  2.1 0.7 copy-done.4
  2.8 0.0 copy-start.5
  2.8 0.7 copy-done.5
  3.5 0.0 copy-start.6
  3.5 0.7 copy-done.6
  4.1 0.0 copy-start.2
  4.1 11.1 %gather_image.1 = (f32[1024,128]{1,0:T(8,128)S(1)}, s32[1,640]{1,0:T(1,128)S(1)}) custom-call(s32[1,1]{1,0:T(1,128)S(6)} %copy.9.count_ref, s32[1,512]{1,0:T(1,128)S(1)} %bitcast.12, s32[1,512]{1,0:T(1,128)S(1)} %bitcast.13, s32[1,128]{1,0:T(1,128)S(1)} %copy-done.6, f32[128,128]{1,0:T(8,128)S(1)} %copy-done), custom_call_target="tpu_custom_call" | custom-call | flops 9200000000 | tf_op jit(solution)/shard_map/gather_image/pallas_call | solution.py:135
  15.2 0.0 copy-done.2
  15.2 0.0 copy-start.3
  15.2 9.6 %forward_tiles.1 = (f32[32,264,128]{2,1,0:T(8,128)S(1)}, f32[8,8,128]{2,1,0:T(8,128)S(1)}) custom-call(s32[1,640]{1,0:T(1,128)S(1)} %get-tuple-element.10.code_ref, f32[16384,128]{1,0:T(8,128)S(1)} %bitcast.9, f32[1024,128]{1,0:T(8,128)S(1)} %get-tuple-element.11.img_ref), custom_call_target="tpu_custom_call" | custom-call | flops 14949999616 | tf_op jit(solution)/shard_map/forward_tiles/pallas_call | solution.py:243
  24.9 0.0 copy-done.3
  24.9 58.7 %sum_and_spread.1 = (f32[256,128]{1,0:T(8,128)S(1)}, f32[32,256,128]{2,1,0:T(8,128)S(1)}) custom-call(f32[32,264,128]{2,1,0:T(8,128)S(1)} %get-tuple-element.12.p_ref, f32[256,128]{1,0:T(8,128)S(1)} %bitcast.11), custom_call_target="tpu_custom_call" | custom-call | flops 57500000256 | tf_op jit(solution)/shard_map/sum_and_spread/pallas_call | solution.py:538
  83.6 8.1 %backward_tiles.1 = (f32[8,136,128]{2,1,0:T(8,128)S(1)}, f32[256,128]{1,0:T(8,128)}) custom-call(s32[1,640]{1,0:T(1,128)S(1)} %get-tuple-element.10.code_ref, f32[16384,128]{1,0:T(8,128)S(1)} %bitcast.10, f32[32,256,128]{2,1,0:T(8,128)S(1)} %get-tuple-element.13.all_ref, f32[8,8,128]{2,1,0:T(8,128)S(1)} %get-tuple-element.14.col_ref, ...), custom_call_target="tpu_custom_call" | custom-call | flops 11500000256 | tf_op jit(solution)/shard_map/backward_tiles/pallas_call | solution.py:600
  91.7 0.0 copy-start.1
  91.7 14.1 %sum_over_angles.1 = f32[128,128]{1,0:T(8,128)S(1)} custom-call(f32[8,136,128]{2,1,0:T(8,128)S(1)} %get-tuple-element.16.b_ref), custom_call_target="tpu_custom_call" | custom-call | flops 8049999872 | tf_op jit(solution)/shard_map/sum_over_angles/pallas_call | solution.py:678
  105.8 0.0 copy-done.1
  105.8 0.6 add.3
Async XLA Ops:
  1.3 0.8 copy-start
  2.1 0.7 copy-start.4
  2.8 0.7 copy-start.5
  3.5 0.7 copy-start.6
  4.1 11.1 %copy-start.2 = (f32[1,1,512,4096]{3,2,1,0:T(8,128)S(1)}, f32[1,1,512,4096]{3,2,1,0:T(8,128)}, u32[]{:S(2)}) copy-start(f32[1,1,512,4096]{3,2,1,0:T(8,128)} %param.7) | copy-start | bytes 25165828
  15.2 9.7 %copy-start.3 = (f32[1,256,128]{2,1,0:T(8,128)S(1)}, f32[1,256,128]{2,1,0:T(8,128)}, u32[]{:S(2)}) copy-start(f32[1,256,128]{2,1,0:T(8,128)} %param.13) | copy-start | bytes 393220
  91.7 14.1 %copy-start.1 = (f32[128,128]{1,0:T(8,128)S(1)}, f32[128,128]{1,0:T(8,128)}, u32[]{:S(2)}) copy-start(f32[128,128]{1,0:T(8,128)} %img_ref.1) | copy-start | bytes 196612

commit v3 on v2

--- a/solution.py
+++ b/solution.py
@@ -50,13 +50,15 @@
         return lax.rem(self.x + dx % NX, NX) * 2 + (1 - self.core)
 
     def device(self, to):
-        return (self.pix, self.twin() if to == "twin" else self.index(to))
-
-    def meet(self):
+        if to == "twin":
+            return (self.pix, self.twin())
+        return (self.pix, self.twin(to // 2) if to % 2 == 0 else self.index(to))
+
+    def meet(self, others):
         barrier = pltpu.get_barrier_semaphore()
-        for to in ("twin", 1, -1):
+        for to in others:
             pl.semaphore_signal(barrier, inc=1, device_id=self.device(to), device_id_type=MESH)
-        pl.semaphore_wait(barrier, 3)
+        pl.semaphore_wait(barrier, len(others))
 
 
 def sort_tiles(ray, pix, used_tiles, table):
@@ -87,10 +89,10 @@
 
 
 def gather_kernel(
-    count_ref, ray_ref, pix_ref, table_ref, img_ref, out_ref, code_ref, send_sem, recv_sem
+    index_ref, img_ref, out_ref, code_ref, send_sem, recv_sem
 ):
     here = Ang()
-    here.meet()
+    here.meet(("twin", 1, -1, 2, -2))
     number = iter(range(13))
 
     def send(to, dx, half, src=None):
@@ -112,33 +114,32 @@
     near = [send(-sign_of(h), 0, h, img_ref) for h in range(2)]
     across = [send("twin", 0, None, img_ref)]
     out_ref[pl.ds(pl.multiple_of(here.me * 128, 128), 128), :] = img_ref[...]
-    code_ref[...] = sort_tiles(ray_ref[...], pix_ref[...], count_ref[0, 0], table_ref[...])
+    ray, pix = index_ref[:, :SLOTS], index_ref[:, SLOTS : 2 * SLOTS]
+    table, used_tiles = index_ref[:, 2 * SLOTS : 2 * SLOTS + RB], index_ref[:, 2 * SLOTS + RB :]
+    code_ref[...] = sort_tiles(ray, pix, used_tiles, table)
     second = []
     for h in range(2):
         far[h].wait_recv()
-        second.append(send(sign_of(h), -sign_of(h), h))
-    for h in range(2):
+        second += [send(sign_of(h), -sign_of(h), h), send(2 * sign_of(h), -sign_of(h), h)]
         across.append(send("twin", -sign_of(h), h))
     for h in range(2):
         near[h].wait_recv()
         across.append(send("twin", sign_of(h), h))
-    for h in range(2):
-        second[h].wait_recv()
-        across.append(send("twin", 2, h))
+    across += second
     for copy in across:
         copy.wait_recv()
-    for copy in far + near + second + across:
+    for copy in far + near + across:
         copy.wait_send()
 
 
-def gather_image(count, ray, pix, table, image):
+def gather_image(index, image):
     return pl.pallas_call(
         gather_kernel,
         out_shape=(
             jax.ShapeDtypeStruct((NA * 128, S), jnp.float32),
             jax.ShapeDtypeStruct((1, NPOS_PAD), jnp.int32),
         ),
-        in_specs=[SM, VM, VM, VM, VM],
+        in_specs=[VM, VM],
         out_specs=(VM, VM),
         scratch_shapes=[
             pltpu.SemaphoreType.DMA((13,)),
@@ -149,7 +150,7 @@
         ),
         cost_estimate=cost(8),
         name="gather_image",
-    )(count, ray, pix, table, image)
+    )(index, image)
 
 
 def tile_rows(tiles_ref, code):
@@ -301,7 +302,7 @@
 
 
 RATE = 95.0
-LATENCY = 1.5
+LATENCY = 2.5
 
 SUM_A = (0, 104)
 SUM_B = (104, 264)
@@ -620,7 +621,7 @@
 
 def update_kernel(b_ref, out_ref, sib, far_buf, near_buf, second_buf, send_sem, recv_sem):
     here = Ang()
-    here.meet()
+    here.meet(("twin", 1, -1))
     number = iter(range(10))
 
     def send(to, src, dst):
@@ -698,7 +699,9 @@
 
 def shards(tiles, tile_ray, tile_pix, tile_count, ray_slot, image, measured):
     rows = tiles[0, 0].reshape(SLOTS // 8, 8, 32, 128).transpose(0, 2, 1, 3).reshape(SLOTS * 32, 128)
-    img, code = gather_image(tile_count, tile_ray[0], tile_pix[0], ray_slot, image)
+    used_tiles = jnp.broadcast_to(tile_count[0], (RB,))
+    index = jnp.concatenate([tile_ray[0, 0], tile_pix[0, 0], ray_slot[0], used_tiles])[None]
+    img, code = gather_image(index, image)
     p, col = forward(code, rows, img)
     own, everyone = exchange(p, measured[0])
     b, resid = backward(code, rows, everyone, col, own)

time: 107 us -> 101 us (0.944)
  Pallas kernels: 102 us -> 97.1 us
  local copies, waits for them, and re-layouts: 2.87 us -> 0.86 us
    pallas_call x1, Pallas kernels: 58.7 us -> 56.5 us  [exchange(): pl.pallas_call(exchange_kernel, out_shape=(jax.ShapeDtypeStruct((OWN, S),...]
    unnamed x14 -> x8, local copies, waits for them, and re-layouts: 2.87 us -> 0.85 us
where the time goes in v3:
time: 101 us
  Pallas kernels  97.1 us (96%)
  other arithmetic  1.36 us (1%)
  between operations  1.36 us (1%)
    pallas_call x1, Pallas kernels, exchange(): pl.pallas_call(exchange_kernel, out_shape=(jax.ShapeDtypeStruct((OWN, S),...  56.5 us
    pallas_call x1, Pallas kernels, update(): pl.pallas_call(update_kernel, out_shape=jax.ShapeDtypeStruct((128, S), jn...  14 us
    pallas_call x1, Pallas kernels, gather_image(): pl.pallas_call(gather_kernel, out_shape=(jax.ShapeDtypeStruct((NA * 128,...  10.3 us
    pallas_call x1, Pallas kernels, forward(): pl.pallas_call(forward_kernel, out_shape=(jax.ShapeDtypeStruct((NZ * NY,...  8.95 us
    pallas_call x1, Pallas kernels, backward(): pl.pallas_call(backward_kernel, out_shape=(jax.ShapeDtypeStruct((NA, 136,...  7.43 us

profile of v3, /device:TPU:1, one launch (start us, length us, event | category | flops | bytes accessed | tf_op | source)
XLA Modules:
  0.0 100.7 jit_solution(17050625106489581146)
XLA Ops:
  1.3 0.7 pad_add_fusion
  2.0 0.0 copy-start
  2.0 0.8 copy-done
  2.9 0.0 copy-start.2
  2.9 10.3 %gather_image.1 = (f32[1024,128]{1,0:T(8,128)S(1)}, s32[1,640]{1,0:T(1,128)S(1)}) custom-call(s32[1,1280]{1,0:T(1,128)S(1)} %broadcast_in_dim.15.index_ref, f32[128,128]{1,0:T(8,128)S(1)} %copy-done), custom_call_target="tpu_custom_call" | custom-call | flops 9200000000 | tf_op jit(solution)/shard_map/gather_image/pallas_call | solution.py:136
  13.2 0.0 copy-done.2
  13.2 0.0 copy-start.3
  13.2 8.9 %forward_tiles.1 = (f32[32,264,128]{2,1,0:T(8,128)S(1)}, f32[8,8,128]{2,1,0:T(8,128)S(1)}) custom-call(s32[1,640]{1,0:T(1,128)S(1)} %get-tuple-element.10.code_ref, f32[16384,128]{1,0:T(8,128)S(1)} %bitcast.12, f32[1024,128]{1,0:T(8,128)S(1)} %get-tuple-element.11.img_ref), custom_call_target="tpu_custom_call" | custom-call | flops 14949999616 | tf_op jit(solution)/shard_map/forward_tiles/pallas_call | solution.py:244
  22.2 0.0 copy-done.3
  22.2 56.5 %sum_and_spread.1 = (f32[256,128]{1,0:T(8,128)S(1)}, f32[32,256,128]{2,1,0:T(8,128)S(1)}) custom-call(f32[32,264,128]{2,1,0:T(8,128)S(1)} %get-tuple-element.12.p_ref, f32[256,128]{1,0:T(8,128)S(1)} %bitcast.14), custom_call_target="tpu_custom_call" | custom-call | flops 57500000256 | tf_op jit(solution)/shard_map/sum_and_spread/pallas_call | solution.py:539
  78.6 7.4 %backward_tiles.1 = (f32[8,136,128]{2,1,0:T(8,128)S(1)}, f32[256,128]{1,0:T(8,128)}) custom-call(s32[1,640]{1,0:T(1,128)S(1)} %get-tuple-element.10.code_ref, f32[16384,128]{1,0:T(8,128)S(1)} %bitcast.13, f32[32,256,128]{2,1,0:T(8,128)S(1)} %get-tuple-element.13.all_ref, f32[8,8,128]{2,1,0:T(8,128)S(1)} %get-tuple-element.14.col_ref, ...), custom_call_target="tpu_custom_call" | custom-call | flops 11500000256 | tf_op jit(solution)/shard_map/backward_tiles/pallas_call | solution.py:601
  86.1 0.0 copy-start.1
  86.1 14.0 %sum_over_angles.1 = f32[128,128]{1,0:T(8,128)S(1)} custom-call(f32[8,136,128]{2,1,0:T(8,128)S(1)} %get-tuple-element.16.b_ref), custom_call_target="tpu_custom_call" | custom-call | flops 8049999872 | tf_op jit(solution)/shard_map/sum_over_angles/pallas_call | solution.py:679
  100.0 0.0 copy-done.1
  100.0 0.6 add.3
  (2 shorter events, 0.0 us)
Async XLA Ops:
  2.0 0.8 copy-start
  2.9 10.3 %copy-start.2 = (f32[1,1,512,4096]{3,2,1,0:T(8,128)S(1)}, f32[1,1,512,4096]{3,2,1,0:T(8,128)}, u32[]{:S(2)}) copy-start(f32[1,1,512,4096]{3,2,1,0:T(8,128)} %param.7) | copy-start | bytes 25165828
  13.2 9.0 %copy-start.3 = (f32[1,256,128]{2,1,0:T(8,128)S(1)}, f32[1,256,128]{2,1,0:T(8,128)}, u32[]{:S(2)}) copy-start(f32[1,256,128]{2,1,0:T(8,128)} %param.13) | copy-start | bytes 393220
  86.1 14.0 %copy-start.1 = (f32[128,128]{1,0:T(8,128)S(1)}, f32[128,128]{1,0:T(8,128)}, u32[]{:S(2)}) copy-start(f32[128,128]{1,0:T(8,128)} %img_ref.1) | copy-start | bytes 196612

commit v4 on v3

--- a/solution.py
+++ b/solution.py
@@ -14,6 +14,9 @@
 GRP = 4
 NPOS = SLOTS + QB * (GRP - 1)
 NPOS_PAD = 640
+LIST = NPOS_PAD + 128
+BWD = 12
+STEPS = NPOS // GRP // BWD + 1
 OWN = 256
 CH = OWN + 8
 VM = pl.BlockSpec(memory_space=pltpu.VMEM)
@@ -58,7 +61,7 @@
         barrier = pltpu.get_barrier_semaphore()
         for to in others:
             pl.semaphore_signal(barrier, inc=1, device_id=self.device(to), device_id_type=MESH)
-        pl.semaphore_wait(barrier, len(others))
+        return lambda: pl.semaphore_wait(barrier, len(others))
 
 
 def sort_tiles(ray, pix, used_tiles, table):
@@ -85,6 +88,7 @@
         at = (lax.broadcasted_iota(jnp.int32, (1, 128), 1) + c * 128).astype(f32)
         part = jnp.sum(jnp.where(place == at, code, 0.0), axis=0, keepdims=True)
         parts.append(jnp.where(at == NPOS_PAD - 1, jnp.sum(groups, axis=1, keepdims=True), part))
+    parts.append(jnp.where(groups > 0.0, first[:1] + groups - 1.0, -1.0))
     return jnp.concatenate(parts, axis=1).astype(jnp.int32)
 
 
@@ -92,7 +96,7 @@
     index_ref, img_ref, out_ref, code_ref, send_sem, recv_sem
 ):
     here = Ang()
-    here.meet(("twin", 1, -1, 2, -2))
+    here.meet(("twin", 1, -1, 2, -2))()
     number = iter(range(13))
 
     def send(to, dx, half, src=None):
@@ -137,7 +141,7 @@
         gather_kernel,
         out_shape=(
             jax.ShapeDtypeStruct((NA * 128, S), jnp.float32),
-            jax.ShapeDtypeStruct((1, NPOS_PAD), jnp.int32),
+            jax.ShapeDtypeStruct((1, LIST), jnp.int32),
         ),
         in_specs=[VM, VM],
         out_specs=(VM, VM),
@@ -163,7 +167,7 @@
 FWD = 12
 
 
-def forward_kernel(code_ref, tiles_ref, img_ref, p_ref, col_ref, w_ref, rowacc, colacc):
+def forward_kernel(code_ref, tiles_ref, img_ref, p_ref, col_ref, turned_ref, w_ref, rowacc, colacc):
     zero = jnp.zeros((BLK, S), jnp.bfloat16)
 
     def weights(q, _):
@@ -205,6 +209,7 @@
             slots = [c & (RB - 1) for c in codes]
             tiles = [tile_rows(tiles_ref, c) for c in codes]
             hi, lo = split_bf16(jnp.concatenate(tiles, axis=0))
+            turned_ref[b * FWD + i] = jnp.concatenate([hi.T, lo.T], axis=1)
             out = jnp.dot(jnp.concatenate([hi, lo, hi], axis=1), w_ref[q], preferred_element_type=jnp.float32)
             terms = [
                 jnp.concatenate([out[32 * j : 32 * j + 32, h * S : h * S + S] for h in range(2)], axis=0)
@@ -246,9 +251,10 @@
         out_shape=(
             jax.ShapeDtypeStruct((NZ * NY, CH, S), jnp.float32),
             jax.ShapeDtypeStruct((NA, 8, 128), jnp.float32),
+            jax.ShapeDtypeStruct((STEPS * BWD, 128, 2 * 128), jnp.bfloat16),
         ),
         in_specs=[SM, VM, VM],
-        out_specs=(VM, VM),
+        out_specs=(VM, VM, VM),
         scratch_shapes=[
             vmem(QB, 6 * BLK, 2 * S, dtype=jnp.bfloat16),
             vmem(RB, 32, 128),
@@ -558,70 +564,54 @@
     )(p, measured)
 
 
-BWD = 12
-
-
-def backward_kernel(code_ref, tiles_ref, all_ref, col_ref, own_ref, b_ref, resid_ref, hi_ref, lo_ref):
-    resid_ref[...] = own_ref[...]
+UPD = ((0, 72), (72, 136))
+
+
+def backward_kernel(
+    code_ref, turned_ref, all_ref, col_ref, out_ref, hi_ref, lo_ref, run_ref, b_ref, sib, far_buf, near_buf, second_buf,
+    send_sem, recv_sem,
+):
+    here = Ang()
+    wait_for_others = here.meet(("twin", 1, -1))
 
     def split(o, _):
-        rows = pl.ds(pl.multiple_of(o * OWN, OWN), OWN)
-        hi_ref[rows, :], lo_ref[rows, :] = split_bf16(all_ref[o])
+        rows = pl.ds(pl.multiple_of(o * 8, 8), 8)
+        hi_ref[rows], lo_ref[rows] = split_bf16(all_ref[o].reshape(8, 32, S))
         return _
 
     lax.fori_loop(0, NZ * NY, split, 0, unroll=2)
-    for o in range(NA):
-        b_ref[o, 0:128, :] = jnp.zeros((128, S), jnp.float32)
-        b_ref[o, 128:136, :] = col_ref[o]
-
-    def step(b, _):
+
+    def pixel_block(g):
+        return lax.shift_right_logical(code_ref[0, g * GRP], 16) & (QB - 1)
+
+    def step(b, run):
         for i in range(BWD):
-            codes = [code_ref[0, (b * BWD + i) * GRP + j] for j in range(GRP)]
-            q = lax.shift_right_logical(codes[0], 16) & (QB - 1)
-            hi, lo = split_bf16(jnp.concatenate([tile_rows(tiles_ref, c) for c in codes], axis=0).T)
-            starts = [(c & (RB - 1)) * BLK for c in codes]
+            g = b * BWD + i
+            codes = [code_ref[0, g * GRP + j] for j in range(GRP)]
+            hi, lo = turned_ref[g, :, :128], turned_ref[g, :, 128:]
+            slots = [c & (RB - 1) for c in codes]
 
             def rays(ref):
-                return [
-                    ref[pl.ds(pl.multiple_of(start + 32 * h, 32), 32), :] for h in range(2) for start in starts
-                ]
+                return [ref[slot * 2 + h] for h in range(2) for slot in slots]
 
             r_hi, r_lo = rays(hi_ref), rays(lo_ref)
             left = jnp.concatenate([hi[:BLK], hi[BLK:], lo[:BLK], lo[BLK:], hi[:BLK], hi[BLK:]], axis=1)
             right = jnp.concatenate(r_hi + r_hi + r_lo, axis=0)
             out = jnp.dot(left, right, preferred_element_type=jnp.float32)
-            rows = pl.ds(pl.multiple_of((q & 1) * BLK, BLK), BLK)
-            b_ref[lax.shift_right_logical(q, 1), rows, :] += out
-        return _
-
-    lax.fori_loop(0, (code_ref[0, NPOS_PAD - 1] + BWD - 1) // BWD, step, 0)
-
-
-def backward(code, tiles, everyone, col, own):
-    return pl.pallas_call(
-        backward_kernel,
-        out_shape=(
-            jax.ShapeDtypeStruct((NA, 136, S), jnp.float32),
-            jax.ShapeDtypeStruct((OWN, S), jnp.float32),
-        ),
-        in_specs=[SM, VM, VM, VM, VM],
-        out_specs=(VM, VM),
-        scratch_shapes=[
-            vmem(RB * BLK, S, dtype=jnp.bfloat16),
-            vmem(RB * BLK, S, dtype=jnp.bfloat16),
-        ],
-        compiler_params=pltpu.CompilerParams(vmem_limit_bytes=32 * MIB),
-        cost_estimate=cost(10),
-        name="backward_tiles",
-    )(code, tiles, everyone, col, own)
-
-
-UPD = ((0, 72), (72, 136))
-
-
-def update_kernel(b_ref, out_ref, sib, far_buf, near_buf, second_buf, send_sem, recv_sem):
-    here = Ang()
-    here.meet(("twin", 1, -1))
+            before = pixel_block(jnp.maximum(g - 1, 0))
+            run = run * (before == pixel_block(g)).astype(jnp.float32) + out
+            run_ref[g] = run
+        return run
+
+    lax.fori_loop(0, STEPS, step, jnp.zeros((BLK, S), jnp.float32))
+    for q in range(QB):
+        last = code_ref[0, NPOS_PAD + q]
+        total = run_ref[jnp.maximum(last, 0)]
+        b_ref[q // 2, q % 2 * BLK : q % 2 * BLK + BLK, :] = total * (last >= 0).astype(jnp.float32)
+    for o in range(NA):
+        b_ref[o, 128:136, :] = col_ref[o]
+
+    wait_for_others()
     number = iter(range(10))
 
     def send(to, src, dst):
@@ -674,14 +664,18 @@
         copy.wait_send()
 
 
-def update(b):
+def backward(code, turned, everyone, col):
     size = UPD[0][1]
     return pl.pallas_call(
-        update_kernel,
+        backward_kernel,
         out_shape=jax.ShapeDtypeStruct((128, S), jnp.float32),
-        in_specs=[VM],
+        in_specs=[SM, VM, VM, VM],
         out_specs=VM,
         scratch_shapes=[
+            vmem(RB * 2, 32, S, dtype=jnp.bfloat16),
+            vmem(RB * 2, 32, S, dtype=jnp.bfloat16),
+            vmem(STEPS * BWD, BLK, S),
+            vmem(NA, 136, S),
             vmem(NX, 136, S),
             vmem(2, size, S),
             vmem(2, size, S),
@@ -690,11 +684,11 @@
             pltpu.SemaphoreType.DMA((10,)),
         ],
         compiler_params=pltpu.CompilerParams(
-            collective_id=2, has_side_effects=True, vmem_limit_bytes=24 * MIB
+            collective_id=2, has_side_effects=True, vmem_limit_bytes=32 * MIB
         ),
-        cost_estimate=cost(7),
-        name="sum_over_angles",
-    )(b)
+        cost_estimate=cost(17),
+        name="backward_and_sum",
+    )(code, turned, everyone, col)
 
 
 def shards(tiles, tile_ray, tile_pix, tile_count, ray_slot, image, measured):
@@ -702,10 +696,9 @@
     used_tiles = jnp.broadcast_to(tile_count[0], (RB,))
     index = jnp.concatenate([tile_ray[0, 0], tile_pix[0, 0], ray_slot[0], used_tiles])[None]
     img, code = gather_image(index, image)
-    p, col = forward(code, rows, img)
+    p, col, turned = forward(code, rows, img)
     own, everyone = exchange(p, measured[0])
-    b, resid = backward(code, rows, everyone, col, own)
-    return (image + update(b), resid[None])
+    return (image + backward(code, turned, everyone, col), own[None])
 
 
 def solution(mesh):

time: 101 us -> 100 us (0.990)
  Pallas kernels: 97.1 us -> 96 us
    pallas_call x1, Pallas kernels: 56.5 us -> 60.7 us  [exchange(): pl.pallas_call(exchange_kernel, out_shape=(jax.ShapeDtypeStruct((OWN, S),...]
    pallas_call x2 -> x1, Pallas kernels: 21.4 us -> 18 us  [backward(): pl.pallas_call(backward_kernel, out_shape=jax.ShapeDtypeStruct((128, S),...]
    pallas_call x1, Pallas kernels: 8.95 us -> 7.01 us  [forward(): pl.pallas_call(forward_kernel, out_shape=(jax.ShapeDtypeStruct((NZ * NY,...]
where the time goes in v4:
time: 100 us
  Pallas kernels  96 us (96%)
  local copies, waits for them, and re-layouts  1.51 us (2%)
  other arithmetic  1.36 us (1%)
  between operations  1.36 us (1%)
    pallas_call x1, Pallas kernels, exchange(): pl.pallas_call(exchange_kernel, out_shape=(jax.ShapeDtypeStruct((OWN, S),...  60.7 us
    pallas_call x1, Pallas kernels, backward(): pl.pallas_call(backward_kernel, out_shape=jax.ShapeDtypeStruct((128, S),...  18 us
    pallas_call x1, Pallas kernels, gather_image(): pl.pallas_call(gather_kernel, out_shape=(jax.ShapeDtypeStruct((NA * 128,...  10.3 us
    pallas_call x1, Pallas kernels, forward(): pl.pallas_call(forward_kernel, out_shape=(jax.ShapeDtypeStruct((NZ * NY,...  7.01 us

profile of v4, /device:TPU:1, one launch (start us, length us, event | category | flops | bytes accessed | tf_op | source)
XLA Modules:
  0.0 100.2 jit_solution(8413701289587649029)
XLA Ops:
  1.3 0.7 pad_add_fusion
  2.0 0.0 copy-start
  2.0 0.8 copy-done
  2.9 0.0 copy-start.2
  2.9 10.3 %gather_image.1 = (f32[1024,128]{1,0:T(8,128)S(1)}, s32[1,768]{1,0:T(1,128)S(1)}) custom-call(s32[1,1280]{1,0:T(1,128)S(1)} %broadcast_in_dim.15.index_ref, f32[128,128]{1,0:T(8,128)S(1)} %copy-done), custom_call_target="tpu_custom_call" | custom-call | flops 9200000000 | tf_op jit(solution)/shard_map/gather_image/pallas_call | solution.py:140
  13.2 0.0 copy-done.2
  13.2 0.0 copy-start.3
  13.2 7.0 %forward_tiles.1 = (f32[32,264,128]{2,1,0:T(8,128)S(1)}, f32[8,8,128]{2,1,0:T(8,128)S(1)}, bf16[144,128,256]{2,1,0:T(8,128)(2,1)S(1)}) custom-call(s32[1,768]{1,0:T(1,128)S(1)} %get-tuple-element.9.code_ref, f32[16384,128]{1,0:T(8,128)S(1)} %bitcast.13, f32[1024,128]{1,0:T(8,128)S(1)} %get-tuple-element.10.img_ref), custom_call_target="tpu_custom_call" | custom-call | flops 14949999616 | tf_op jit(solution)/shard_map/forward_tiles/pallas_call | solution.py:249
  20.2 0.0 copy-done.3
  20.2 60.7 %sum_and_spread.1 = (f32[256,128]{1,0:T(8,128)S(1)}, f32[32,256,128]{2,1,0:T(8,128)S(1)}) custom-call(f32[32,264,128]{2,1,0:T(8,128)S(1)} %get-tuple-element.12.p_ref, f32[256,128]{1,0:T(8,128)S(1)} %bitcast.14), custom_call_target="tpu_custom_call" | custom-call | flops 57500000256 | tf_op jit(solution)/shard_map/sum_and_spread/pallas_call | solution.py:545
  81.0 0.0 copy-start.1
  81.0 18.0 %backward_and_sum.1 = f32[128,128]{1,0:T(8,128)S(1)} custom-call(s32[1,768]{1,0:T(1,128)S(1)} %get-tuple-element.9.code_ref, bf16[144,128,256]{2,1,0:T(8,128)(2,1)S(1)} %get-tuple-element.11.turned_ref, f32[32,256,128]{2,1,0:T(8,128)S(1)} %get-tuple-element.13.all_ref, f32[8,8,128]{2,1,0:T(8,128)S(1)} %get-tuple-element.14.col_ref), custom_call_target="tpu_custom_call" | custom-call | flops 19549999104 | tf_op jit(solution)/shard_map/backward_and_sum/pallas_call | solution.py:669
  98.9 0.0 copy-done.1
  98.9 0.6 add.3
  99.6 0.7 copy.11
  (2 shorter events, 0.0 us)
Async XLA Ops:
  2.0 0.8 copy-start
  2.9 10.3 %copy-start.2 = (f32[1,1,512,4096]{3,2,1,0:T(8,128)S(1)}, f32[1,1,512,4096]{3,2,1,0:T(8,128)}, u32[]{:S(2)}) copy-start(f32[1,1,512,4096]{3,2,1,0:T(8,128)} %param.7) | copy-start | bytes 25165828
  13.2 7.0 %copy-start.3 = (f32[1,256,128]{2,1,0:T(8,128)S(1)}, f32[1,256,128]{2,1,0:T(8,128)}, u32[]{:S(2)}) copy-start(f32[1,256,128]{2,1,0:T(8,128)} %param.13) | copy-start | bytes 393220
  81.0 18.0 %copy-start.1 = (f32[128,128]{1,0:T(8,128)S(1)}, f32[128,128]{1,0:T(8,128)}, u32[]{:S(2)}) copy-start(f32[128,128]{1,0:T(8,128)} %img_ref.1) | copy-start | bytes 196612

commit v5 on v4

--- a/solution.py
+++ b/solution.py
@@ -377,7 +377,9 @@
 AHEAD = 3
 
 
-def exchange_kernel(p_ref, meas_ref, resid_ref, all_ref, ra1, ra2, rb1, rb2, own, send_sem, recv_sem):
+def exchange_kernel(
+    p_ref, meas_ref, resid_ref, hi_ref, lo_ref, all_ref, ra1, ra2, rb1, rb2, own, send_sem, recv_sem
+):
     pix, ang = lax.axis_index("pix"), lax.axis_index("ang")
     z, y = pix // NY, lax.rem(pix, NY)
 
@@ -527,8 +529,39 @@
             resid_ref[natural, :] = value
             all_ref[at(0, 0), mine, :] = value
 
+    def place(key):
+        stage, piece, chain, s = key
+        d, _ = chain_of(NY if stage in ("c1", "d2") else NZ, piece, chain)
+        off = -d * s
+        if stage == "c1":
+            return 0, off % NY
+        if stage == "d1":
+            return off % NZ, 0
+        return (off % NZ, piece) if stage == "c2" else (piece, off % NY)
+
+    parts = {}
     for key in alls:
+        parts.setdefault(place(key), []).append(key)
+
+    def split(where):
+        o = at(*where)
+        rows = pl.ds(pl.multiple_of(o * 8, 8), 8)
+        hi_ref[rows], lo_ref[rows] = split_bf16(all_ref[o].reshape(8, 32, S))
+
+    def split_whole():
+        for where in list(parts):
+            if all(k in received for k in parts[where]):
+                del parts[where]
+                split(where)
+
+    for i, key in enumerate(alls):
         issue(key)
+        if i == 8:
+            split((0, 0))
+        split_whole()
+    for key in alls:
+        receive(key)
+        split_whole()
     for t in tasks:
         receive(t.key)
     for t in tasks:
@@ -546,11 +579,13 @@
         exchange_kernel,
         out_shape=(
             jax.ShapeDtypeStruct((OWN, S), jnp.float32),
-            jax.ShapeDtypeStruct((NZ * NY, OWN, S), jnp.float32),
+            jax.ShapeDtypeStruct((RB * 2, 32, S), jnp.bfloat16),
+            jax.ShapeDtypeStruct((RB * 2, 32, S), jnp.bfloat16),
         ),
         in_specs=[VM, VM],
-        out_specs=(VM, VM),
-        scratch_shapes=[vmem(count[k], most[k], S) for k in ("a1", "a2", "b1", "b2")]
+        out_specs=(VM, VM, VM),
+        scratch_shapes=[vmem(NZ * NY, OWN, S)]
+        + [vmem(count[k], most[k], S) for k in ("a1", "a2", "b1", "b2")]
         + [
             vmem(CH, S),
             pltpu.SemaphoreType.DMA((len(tasks),)),
@@ -568,18 +603,11 @@
 
 
 def backward_kernel(
-    code_ref, turned_ref, all_ref, col_ref, out_ref, hi_ref, lo_ref, run_ref, b_ref, sib, far_buf, near_buf, second_buf,
+    code_ref, turned_ref, hi_ref, lo_ref, col_ref, out_ref, run_ref, b_ref, sib, far_buf, near_buf, second_buf,
     send_sem, recv_sem,
 ):
     here = Ang()
     wait_for_others = here.meet(("twin", 1, -1))
-
-    def split(o, _):
-        rows = pl.ds(pl.multiple_of(o * 8, 8), 8)
-        hi_ref[rows], lo_ref[rows] = split_bf16(all_ref[o].reshape(8, 32, S))
-        return _
-
-    lax.fori_loop(0, NZ * NY, split, 0, unroll=2)
 
     def pixel_block(g):
         return lax.shift_right_logical(code_ref[0, g * GRP], 16) & (QB - 1)
@@ -664,16 +692,14 @@
         copy.wait_send()
 
 
-def backward(code, turned, everyone, col):
+def backward(code, turned, high, low, col):
     size = UPD[0][1]
     return pl.pallas_call(
         backward_kernel,
         out_shape=jax.ShapeDtypeStruct((128, S), jnp.float32),
-        in_specs=[SM, VM, VM, VM],
+        in_specs=[SM, VM, VM, VM, VM],
         out_specs=VM,
         scratch_shapes=[
-            vmem(RB * 2, 32, S, dtype=jnp.bfloat16),
-            vmem(RB * 2, 32, S, dtype=jnp.bfloat16),
             vmem(STEPS * BWD, BLK, S),
             vmem(NA, 136, S),
             vmem(NX, 136, S),
@@ -688,7 +714,7 @@
         ),
         cost_estimate=cost(17),
         name="backward_and_sum",
-    )(code, turned, everyone, col)
+    )(code, turned, high, low, col)
 
 
 def shards(tiles, tile_ray, tile_pix, tile_count, ray_slot, image, measured):
@@ -697,8 +723,8 @@
     index = jnp.concatenate([tile_ray[0, 0], tile_pix[0, 0], ray_slot[0], used_tiles])[None]
     img, code = gather_image(index, image)
     p, col, turned = forward(code, rows, img)
-    own, everyone = exchange(p, measured[0])
-    return (image + backward(code, turned, everyone, col), own[None])
+    own, high, low = exchange(p, measured[0])
+    return (image + backward(code, turned, high, low, col), own[None])
 
 
 def solution(mesh):

time: 100 us -> 100 us (level)
    pallas_call x1, Pallas kernels: 60.7 us -> 57.7 us  [exchange(): pl.pallas_call(exchange_kernel, out_shape=(jax.ShapeDtypeStruct((OWN, S),...]
    pallas_call x1, Pallas kernels: 7.01 us -> 9.16 us  [forward(): pl.pallas_call(forward_kernel, out_shape=(jax.ShapeDtypeStruct((NZ * NY,...]
where the time goes in v5:
time: 100 us
  Pallas kernels  96 us (96%)
  local copies, waits for them, and re-layouts  1.51 us (2%)
  other arithmetic  1.36 us (1%)
  between operations  1.36 us (1%)
    pallas_call x1, Pallas kernels, exchange(): pl.pallas_call(exchange_kernel, out_shape=(jax.ShapeDtypeStruct((OWN, S),...  57.7 us
    pallas_call x1, Pallas kernels, backward(): pl.pallas_call(backward_kernel, out_shape=jax.ShapeDtypeStruct((128, S),...  18.9 us
    pallas_call x1, Pallas kernels, gather_image(): pl.pallas_call(gather_kernel, out_shape=(jax.ShapeDtypeStruct((NA * 128,...  10.3 us
    pallas_call x1, Pallas kernels, forward(): pl.pallas_call(forward_kernel, out_shape=(jax.ShapeDtypeStruct((NZ * NY,...  9.16 us

profile of v5, /device:TPU:1, one launch (start us, length us, event | category | flops | bytes accessed | tf_op | source)
XLA Modules:
  0.0 100.3 jit_solution(7515123581384255232)
XLA Ops:
  1.3 0.7 pad_add_fusion
  2.0 0.0 copy-start
  2.0 0.8 copy-done
  2.9 0.0 copy-start.2
  2.9 10.3 %gather_image.1 = (f32[1024,128]{1,0:T(8,128)S(1)}, s32[1,768]{1,0:T(1,128)S(1)}) custom-call(s32[1,1280]{1,0:T(1,128)S(1)} %broadcast_in_dim.15.index_ref, f32[128,128]{1,0:T(8,128)S(1)} %copy-done), custom_call_target="tpu_custom_call" | custom-call | flops 9200000000 | tf_op jit(solution)/shard_map/gather_image/pallas_call | solution.py:140
  13.2 0.0 copy-done.2
  13.2 0.0 copy-start.3
  13.2 9.2 %forward_tiles.1 = (f32[32,264,128]{2,1,0:T(8,128)S(1)}, f32[8,8,128]{2,1,0:T(8,128)S(1)}, bf16[144,128,256]{2,1,0:T(8,128)(2,1)S(1)}) custom-call(s32[1,768]{1,0:T(1,128)S(1)} %get-tuple-element.10.code_ref, f32[16384,128]{1,0:T(8,128)S(1)} %bitcast.13, f32[1024,128]{1,0:T(8,128)S(1)} %get-tuple-element.11.img_ref), custom_call_target="tpu_custom_call" | custom-call | flops 14949999616 | tf_op jit(solution)/shard_map/forward_tiles/pallas_call | solution.py:249
  22.4 0.0 copy-done.3
  22.4 57.7 %sum_and_spread.1 = (f32[256,128]{1,0:T(8,128)S(1)}, bf16[256,32,128]{2,1,0:T(8,128)(2,1)S(1)}, bf16[256,32,128]{2,1,0:T(8,128)(2,1)S(1)}) custom-call(f32[32,264,128]{2,1,0:T(8,128)S(1)} %get-tuple-element.13.p_ref, f32[256,128]{1,0:T(8,128)S(1)} %bitcast.14), custom_call_target="tpu_custom_call" | custom-call | flops 57500000256 | tf_op jit(solution)/shard_map/sum_and_spread/pallas_call | solution.py:578
  80.1 0.0 copy-start.1
  80.1 18.9 %backward_and_sum.1 = f32[128,128]{1,0:T(8,128)S(1)} custom-call(s32[1,768]{1,0:T(1,128)S(1)} %get-tuple-element.10.code_ref, bf16[144,128,256]{2,1,0:T(8,128)(2,1)S(1)} %get-tuple-element.12.turned_ref, bf16[256,32,128]{2,1,0:T(8,128)(2,1)S(1)} %get-tuple-element.14.hi_ref, bf16[256,32,128]{2,1,0:T(8,128)(2,1)S(1)} %get-tuple-element.15.lo_ref, ...), custom_call_target="tpu_custom_call" | custom-call | flops 19549999104 | tf_op jit(solution)/shard_map/backward_and_sum/pallas_call | solution.py:697
  99.0 0.0 copy-done.1
  99.0 0.6 add.3
  99.6 0.7 copy.11
  (2 shorter events, 0.0 us)
Async XLA Ops:
  2.0 0.8 copy-start
  2.9 10.3 %copy-start.2 = (f32[1,1,512,4096]{3,2,1,0:T(8,128)S(1)}, f32[1,1,512,4096]{3,2,1,0:T(8,128)}, u32[]{:S(2)}) copy-start(f32[1,1,512,4096]{3,2,1,0:T(8,128)} %param.7) | copy-start | bytes 25165828
  13.2 9.2 %copy-start.3 = (f32[1,256,128]{2,1,0:T(8,128)S(1)}, f32[1,256,128]{2,1,0:T(8,128)}, u32[]{:S(2)}) copy-start(f32[1,256,128]{2,1,0:T(8,128)} %param.13) | copy-start | bytes 393220
  80.1 18.9 %copy-start.1 = (f32[128,128]{1,0:T(8,128)S(1)}, f32[128,128]{1,0:T(8,128)}, u32[]{:S(2)}) copy-start(f32[128,128]{1,0:T(8,128)} %img_ref.1) | copy-start | bytes 196612

commit v6 on v5

--- a/solution.py
+++ b/solution.py
@@ -224,18 +224,18 @@
 
     lax.fori_loop(0, (code_ref[0, NPOS_PAD - 1] + FWD - 1) // FWD, step, 0)
 
-    pick = lax.broadcasted_iota(jnp.int32, (8, 128), 0) == (lax.broadcasted_iota(jnp.int32, (8, 128), 1) // BLK)
+    lane = lax.broadcasted_iota(jnp.int32, (8, 256), 1)
+    pick = lax.broadcasted_iota(jnp.int32, (8, 256), 0) == (lane & 127) // BLK
     pick = pick.astype(jnp.float32).astype(jnp.bfloat16)
 
     def row_sums(o, _):
-        hi, lo = split_bf16(rowacc[pl.ds(o * 4, 4)].reshape(128, 128))
-        dims = (((1,), (1,)), ((), ()))
-        sums = lax.dot_general(pick, hi, dims, preferred_element_type=jnp.float32)
-        sums += lax.dot_general(pick, lo, dims, preferred_element_type=jnp.float32)
-        p_ref[o, OWN:CH, :] = sums
+        both = jnp.concatenate(split_bf16(rowacc[pl.ds(o * 8, 8)].reshape(256, 128)), axis=1)
+        sums = lax.dot_general(pick, both, (((1,), (1,)), ((), ())), preferred_element_type=jnp.float32)
+        p_ref[2 * o, OWN:CH, :] = sums[:, :128]
+        p_ref[2 * o + 1, OWN:CH, :] = sums[:, 128:]
         return _
 
-    lax.fori_loop(0, NZ * NY, row_sums, 0, unroll=16)
+    lax.fori_loop(0, NZ * NY // 2, row_sums, 0, unroll=8)
     low = lax.broadcasted_iota(jnp.int32, (1, 128), 1) < BLK
     for o in range(NA):
         a = jnp.sum(colacc[2 * o], axis=0, keepdims=True)
@@ -717,6 +717,26 @@
     )(code, turned, high, low, col)
 
 
+def finish_kernel(image_ref, step_ref, own_ref, new_ref, resid_ref):
+    resid_ref[...] = own_ref[...]
+    new_ref[...] = image_ref[...] + step_ref[...]
+
+
+def finish(image, step, own):
+    return pl.pallas_call(
+        finish_kernel,
+        out_shape=(
+            jax.ShapeDtypeStruct((128, S), jnp.float32),
+            jax.ShapeDtypeStruct((OWN, S), jnp.float32),
+        ),
+        in_specs=[VM, VM, VM],
+        out_specs=(VM, VM),
+        compiler_params=pltpu.CompilerParams(vmem_limit_bytes=24 * MIB),
+        cost_estimate=cost(1),
+        name="new_image",
+    )(image, step, own)
+
+
 def shards(tiles, tile_ray, tile_pix, tile_count, ray_slot, image, measured):
     rows = tiles[0, 0].reshape(SLOTS // 8, 8, 32, 128).transpose(0, 2, 1, 3).reshape(SLOTS * 32, 128)
     used_tiles = jnp.broadcast_to(tile_count[0], (RB,))
@@ -724,7 +744,8 @@
     img, code = gather_image(index, image)
     p, col, turned = forward(code, rows, img)
     own, high, low = exchange(p, measured[0])
-    return (image + backward(code, turned, high, low, col), own[None])
+    new_image, resid = finish(image, backward(code, turned, high, low, col), own)
+    return (new_image, resid[None])
 
 
 def solution(mesh):

time: 100 us -> 98.4 us (0.984)
    pallas_call x1, Pallas kernels: 9.16 us -> 7.17 us  [forward(): pl.pallas_call(forward_kernel, out_shape=(jax.ShapeDtypeStruct((NZ * NY,...]
    pallas_call x1, Pallas kernels: 57.7 us -> 59.3 us  [exchange(): pl.pallas_call(exchange_kernel, out_shape=(jax.ShapeDtypeStruct((OWN, S),...]
    pallas_call x1, Pallas kernels: 18.9 us -> 17.8 us  [backward(): pl.pallas_call(backward_kernel, out_shape=jax.ShapeDtypeStruct((128, S),...]
where the time goes in v6:
time: 98.4 us; the launch traced here: 98.2 us
  Pallas kernels  95.2 us (97%)
  between operations  1.36 us (1%)
    pallas_call x1, Pallas kernels, exchange(): pl.pallas_call(exchange_kernel, out_shape=(jax.ShapeDtypeStruct((OWN, S),...  59.3 us
    pallas_call x1, Pallas kernels, backward(): pl.pallas_call(backward_kernel, out_shape=jax.ShapeDtypeStruct((128, S),...  17.8 us
    pallas_call x1, Pallas kernels, gather_image(): pl.pallas_call(gather_kernel, out_shape=(jax.ShapeDtypeStruct((NA * 128,...  10.3 us
    pallas_call x1, Pallas kernels, forward(): pl.pallas_call(forward_kernel, out_shape=(jax.ShapeDtypeStruct((NZ * NY,...  7.17 us

profile of v6, /device:TPU:1, one launch (start us, length us, event | category | flops | bytes accessed | tf_op | source)
XLA Modules:
  0.0 98.2 jit_solution(12814871404394462564)
XLA Ops:
  1.3 0.7 pad_add_fusion
  2.0 0.0 copy-start.2
  2.0 0.8 copy-done.2
  2.9 0.0 copy-start
  2.9 10.3 %gather_image.1 = (f32[1024,128]{1,0:T(8,128)S(1)}, s32[1,768]{1,0:T(1,128)S(1)}) custom-call(s32[1,1280]{1,0:T(1,128)S(1)} %broadcast_in_dim.15.index_ref, f32[128,128]{1,0:T(8,128)S(1)} %copy-done.2), custom_call_target="tpu_custom_call" | custom-call | flops 9200000000 | tf_op jit(solution)/shard_map/gather_image/pallas_call | solution.py:140
  13.2 0.0 copy-done
  13.2 0.0 copy-start.1
  13.2 7.2 %forward_tiles.1 = (f32[32,264,128]{2,1,0:T(8,128)S(1)}, f32[8,8,128]{2,1,0:T(8,128)S(1)}, bf16[144,128,256]{2,1,0:T(8,128)(2,1)S(1)}) custom-call(s32[1,768]{1,0:T(1,128)S(1)} %get-tuple-element.12.code_ref, f32[16384,128]{1,0:T(8,128)S(1)} %bitcast.12, f32[1024,128]{1,0:T(8,128)S(1)} %get-tuple-element.13.img_ref), custom_call_target="tpu_custom_call" | custom-call | flops 14949999616 | tf_op jit(solution)/shard_map/forward_tiles/pallas_call | solution.py:249
  20.4 0.0 copy-done.1
  20.4 59.3 %sum_and_spread.1 = (f32[256,128]{1,0:T(8,128)S(1)}, bf16[256,32,128]{2,1,0:T(8,128)(2,1)S(1)}, bf16[256,32,128]{2,1,0:T(8,128)(2,1)S(1)}) custom-call(f32[32,264,128]{2,1,0:T(8,128)S(1)} %get-tuple-element.15.p_ref, f32[256,128]{1,0:T(8,128)S(1)} %bitcast.13), custom_call_target="tpu_custom_call" | custom-call | flops 57500000256 | tf_op jit(solution)/shard_map/sum_and_spread/pallas_call | solution.py:578
  79.7 0.0 copy-start.3
  79.7 17.8 %backward_and_sum.1.step_ref = f32[128,128]{1,0:T(8,128)S(1)} custom-call(s32[1,768]{1,0:T(1,128)S(1)} %get-tuple-element.12.code_ref, bf16[144,128,256]{2,1,0:T(8,128)(2,1)S(1)} %get-tuple-element.14.turned_ref, bf16[256,32,128]{2,1,0:T(8,128)(2,1)S(1)} %get-tuple-element.16.hi_ref, bf16[256,32,128]{2,1,0:T(8,128)(2,1)S(1)} %get-tuple-element.17.lo_ref, ...), custom_call_target="tpu_custom_call" | custom-call | flops 19549999104 | tf_op jit(solution)/shard_map/backward_and_sum/pallas_call | solution.py:697
  97.5 0.0 copy-done.3
  97.5 0.7 new_image.1
  (2 shorter events, 0.0 us)
Async XLA Ops:
  2.0 0.8 copy-start.2
  2.9 10.3 %copy-start = (f32[1,1,512,4096]{3,2,1,0:T(8,128)S(1)}, f32[1,1,512,4096]{3,2,1,0:T(8,128)}, u32[]{:S(2)}) copy-start(f32[1,1,512,4096]{3,2,1,0:T(8,128)} %param.7) | copy-start | bytes 25165828
  13.2 7.2 %copy-start.1 = (f32[1,256,128]{2,1,0:T(8,128)S(1)}, f32[1,256,128]{2,1,0:T(8,128)}, u32[]{:S(2)}) copy-start(f32[1,256,128]{2,1,0:T(8,128)} %param.13) | copy-start | bytes 393220
  79.7 17.8 %copy-start.3 = (f32[128,128]{1,0:T(8,128)S(1)}, f32[128,128]{1,0:T(8,128)}, u32[]{:S(2)}) copy-start(f32[128,128]{1,0:T(8,128)} %image_ref.1) | copy-start | bytes 196612

commit v7 on v6

--- a/solution.py
+++ b/solution.py
@@ -15,7 +15,7 @@
 NPOS = SLOTS + QB * (GRP - 1)
 NPOS_PAD = 640
 LIST = NPOS_PAD + 128
-BWD = 12
+BWD = 18
 STEPS = NPOS // GRP // BWD + 1
 OWN = 256
 CH = OWN + 8
@@ -164,7 +164,7 @@
     return tiles_ref[pl.ds(start, 32, stride=8), :] * used
 
 
-FWD = 12
+FWD = 16
 
 
 def forward_kernel(code_ref, tiles_ref, img_ref, p_ref, col_ref, turned_ref, w_ref, rowacc, colacc):

time: 98.4 us -> 97.5 us (level)
    pallas_call x1, Pallas kernels: 7.17 us -> 9.75 us  [forward(): pl.pallas_call(forward_kernel, out_shape=(jax.ShapeDtypeStruct((NZ * NY,...]
    pallas_call x1, Pallas kernels: 17.8 us -> 15.5 us  [backward(): pl.pallas_call(backward_kernel, out_shape=jax.ShapeDtypeStruct((128, S),...]
    pallas_call x1, Pallas kernels: 59.3 us -> 58.1 us  [exchange(): pl.pallas_call(exchange_kernel, out_shape=(jax.ShapeDtypeStruct((OWN, S),...]
where the time goes in v7:
time: 97.5 us; the launch traced here: 97.3 us
  Pallas kernels  94.4 us (97%)
  between operations  1.36 us (1%)
    pallas_call x1, Pallas kernels, exchange(): pl.pallas_call(exchange_kernel, out_shape=(jax.ShapeDtypeStruct((OWN, S),...  58.1 us
    pallas_call x1, Pallas kernels, backward(): pl.pallas_call(backward_kernel, out_shape=jax.ShapeDtypeStruct((128, S),...  15.5 us
    pallas_call x1, Pallas kernels, gather_image(): pl.pallas_call(gather_kernel, out_shape=(jax.ShapeDtypeStruct((NA * 128,...  10.3 us
    pallas_call x1, Pallas kernels, forward(): pl.pallas_call(forward_kernel, out_shape=(jax.ShapeDtypeStruct((NZ * NY,...  9.75 us

profile of v7, /device:TPU:1, one launch (start us, length us, event | category | flops | bytes accessed | tf_op | source)
XLA Modules:
  0.0 97.3 jit_solution(14521632603452689146)
XLA Ops:
  1.3 0.7 pad_add_fusion
  2.0 0.0 copy-start.2
  2.0 0.8 copy-done.2
  2.9 0.0 copy-start
  2.9 10.3 %gather_image.1 = (f32[1024,128]{1,0:T(8,128)S(1)}, s32[1,768]{1,0:T(1,128)S(1)}) custom-call(s32[1,1280]{1,0:T(1,128)S(1)} %broadcast_in_dim.15.index_ref, f32[128,128]{1,0:T(8,128)S(1)} %copy-done.2), custom_call_target="tpu_custom_call" | custom-call | flops 9200000000 | tf_op jit(solution)/shard_map/gather_image/pallas_call | solution.py:140
  13.2 0.0 copy-done
  13.2 0.0 copy-start.1
  13.2 9.8 %forward_tiles.1 = (f32[32,264,128]{2,1,0:T(8,128)S(1)}, f32[8,8,128]{2,1,0:T(8,128)S(1)}, bf16[144,128,256]{2,1,0:T(8,128)(2,1)S(1)}) custom-call(s32[1,768]{1,0:T(1,128)S(1)} %get-tuple-element.12.code_ref, f32[16384,128]{1,0:T(8,128)S(1)} %bitcast.12, f32[1024,128]{1,0:T(8,128)S(1)} %get-tuple-element.13.img_ref), custom_call_target="tpu_custom_call" | custom-call | flops 14949999616 | tf_op jit(solution)/shard_map/forward_tiles/pallas_call | solution.py:249
  23.0 0.0 copy-done.1
  23.0 58.1 %sum_and_spread.1 = (f32[256,128]{1,0:T(8,128)S(1)}, bf16[256,32,128]{2,1,0:T(8,128)(2,1)S(1)}, bf16[256,32,128]{2,1,0:T(8,128)(2,1)S(1)}) custom-call(f32[32,264,128]{2,1,0:T(8,128)S(1)} %get-tuple-element.15.p_ref, f32[256,128]{1,0:T(8,128)S(1)} %bitcast.13), custom_call_target="tpu_custom_call" | custom-call | flops 57500000256 | tf_op jit(solution)/shard_map/sum_and_spread/pallas_call | solution.py:578
  81.1 0.0 copy-start.3
  81.1 15.5 %backward_and_sum.1.step_ref = f32[128,128]{1,0:T(8,128)S(1)} custom-call(s32[1,768]{1,0:T(1,128)S(1)} %get-tuple-element.12.code_ref, bf16[144,128,256]{2,1,0:T(8,128)(2,1)S(1)} %get-tuple-element.14.turned_ref, bf16[256,32,128]{2,1,0:T(8,128)(2,1)S(1)} %get-tuple-element.16.hi_ref, bf16[256,32,128]{2,1,0:T(8,128)(2,1)S(1)} %get-tuple-element.17.lo_ref, ...), custom_call_target="tpu_custom_call" | custom-call | flops 19549999104 | tf_op jit(solution)/shard_map/backward_and_sum/pallas_call | solution.py:697
  96.6 0.0 copy-done.3
  96.6 0.7 new_image.1
  (2 shorter events, 0.0 us)
Async XLA Ops:
  2.0 0.8 copy-start.2
  2.9 10.3 %copy-start = (f32[1,1,512,4096]{3,2,1,0:T(8,128)S(1)}, f32[1,1,512,4096]{3,2,1,0:T(8,128)}, u32[]{:S(2)}) copy-start(f32[1,1,512,4096]{3,2,1,0:T(8,128)} %param.7) | copy-start | bytes 25165828
  13.2 9.8 %copy-start.1 = (f32[1,256,128]{2,1,0:T(8,128)S(1)}, f32[1,256,128]{2,1,0:T(8,128)}, u32[]{:S(2)}) copy-start(f32[1,256,128]{2,1,0:T(8,128)} %param.13) | copy-start | bytes 393220
  81.1 15.5 %copy-start.3 = (f32[128,128]{1,0:T(8,128)S(1)}, f32[128,128]{1,0:T(8,128)}, u32[]{:S(2)}) copy-start(f32[128,128]{1,0:T(8,128)} %image_ref.1) | copy-start | bytes 196612

commit v8 on v7

--- a/solution.py
+++ b/solution.py
@@ -15,7 +15,7 @@
 NPOS = SLOTS + QB * (GRP - 1)
 NPOS_PAD = 640
 LIST = NPOS_PAD + 128
-BWD = 18
+BWD = 36
 STEPS = NPOS // GRP // BWD + 1
 OWN = 256
 CH = OWN + 8
@@ -164,7 +164,7 @@
     return tiles_ref[pl.ds(start, 32, stride=8), :] * used
 
 
-FWD = 16
+FWD = 24
 
 
 def forward_kernel(code_ref, tiles_ref, img_ref, p_ref, col_ref, turned_ref, w_ref, rowacc, colacc):

time: 97.5 us -> 96.9 us (level)
    pallas_call x1, Pallas kernels: 9.75 us -> 7.45 us  [forward(): pl.pallas_call(forward_kernel, out_shape=(jax.ShapeDtypeStruct((NZ * NY,...]
    pallas_call x1, Pallas kernels: 15.5 us -> 17.3 us  [backward(): pl.pallas_call(backward_kernel, out_shape=jax.ShapeDtypeStruct((128, S),...]
where the time goes in v8:
time: 96.9 us; the launch traced here: 97.2 us
  Pallas kernels  94.2 us (97%)
  between operations  1.36 us (1%)
    pallas_call x1, Pallas kernels, exchange(): pl.pallas_call(exchange_kernel, out_shape=(jax.ShapeDtypeStruct((OWN, S),...  58.5 us
    pallas_call x1, Pallas kernels, backward(): pl.pallas_call(backward_kernel, out_shape=jax.ShapeDtypeStruct((128, S),...  17.3 us
    pallas_call x1, Pallas kernels, gather_image(): pl.pallas_call(gather_kernel, out_shape=(jax.ShapeDtypeStruct((NA * 128,...  10.3 us
    pallas_call x1, Pallas kernels, forward(): pl.pallas_call(forward_kernel, out_shape=(jax.ShapeDtypeStruct((NZ * NY,...  7.45 us

profile of v8, /device:TPU:1, one launch (start us, length us, event | category | flops | bytes accessed | tf_op | source)
XLA Modules:
  0.0 97.2 jit_solution(9215209048224779373)
XLA Ops:
  1.3 0.7 pad_add_fusion
  2.0 0.0 copy-start.2
  2.0 0.8 copy-done.2
  2.9 0.0 copy-start
  2.9 10.3 %gather_image.1 = (f32[1024,128]{1,0:T(8,128)S(1)}, s32[1,768]{1,0:T(1,128)S(1)}) custom-call(s32[1,1280]{1,0:T(1,128)S(1)} %broadcast_in_dim.15.index_ref, f32[128,128]{1,0:T(8,128)S(1)} %copy-done.2), custom_call_target="tpu_custom_call" | custom-call | flops 9200000000 | tf_op jit(solution)/shard_map/gather_image/pallas_call | solution.py:140
  13.2 0.0 copy-done
  13.2 0.0 copy-start.1
  13.2 7.5 %forward_tiles.1 = (f32[32,264,128]{2,1,0:T(8,128)S(1)}, f32[8,8,128]{2,1,0:T(8,128)S(1)}, bf16[144,128,256]{2,1,0:T(8,128)(2,1)S(1)}) custom-call(s32[1,768]{1,0:T(1,128)S(1)} %get-tuple-element.12.code_ref, f32[16384,128]{1,0:T(8,128)S(1)} %bitcast.12, f32[1024,128]{1,0:T(8,128)S(1)} %get-tuple-element.13.img_ref), custom_call_target="tpu_custom_call" | custom-call | flops 14949999616 | tf_op jit(solution)/shard_map/forward_tiles/pallas_call | solution.py:249
  20.7 0.0 copy-done.1
  20.7 58.5 %sum_and_spread.1 = (f32[256,128]{1,0:T(8,128)S(1)}, bf16[256,32,128]{2,1,0:T(8,128)(2,1)S(1)}, bf16[256,32,128]{2,1,0:T(8,128)(2,1)S(1)}) custom-call(f32[32,264,128]{2,1,0:T(8,128)S(1)} %get-tuple-element.15.p_ref, f32[256,128]{1,0:T(8,128)S(1)} %bitcast.13), custom_call_target="tpu_custom_call" | custom-call | flops 57500000256 | tf_op jit(solution)/shard_map/sum_and_spread/pallas_call | solution.py:578
  79.2 0.0 copy-start.3
  79.2 17.3 %backward_and_sum.1.step_ref = f32[128,128]{1,0:T(8,128)S(1)} custom-call(s32[1,768]{1,0:T(1,128)S(1)} %get-tuple-element.12.code_ref, bf16[144,128,256]{2,1,0:T(8,128)(2,1)S(1)} %get-tuple-element.14.turned_ref, bf16[256,32,128]{2,1,0:T(8,128)(2,1)S(1)} %get-tuple-element.16.hi_ref, bf16[256,32,128]{2,1,0:T(8,128)(2,1)S(1)} %get-tuple-element.17.lo_ref, ...), custom_call_target="tpu_custom_call" | custom-call | flops 19549999104 | tf_op jit(solution)/shard_map/backward_and_sum/pallas_call | solution.py:697
  96.5 0.0 copy-done.3
  96.5 0.7 new_image.1
  (2 shorter events, 0.0 us)
Async XLA Ops:
  2.0 0.8 copy-start.2
  2.9 10.3 %copy-start = (f32[1,1,512,4096]{3,2,1,0:T(8,128)S(1)}, f32[1,1,512,4096]{3,2,1,0:T(8,128)}, u32[]{:S(2)}) copy-start(f32[1,1,512,4096]{3,2,1,0:T(8,128)} %param.7) | copy-start | bytes 25165828
  13.2 7.5 %copy-start.1 = (f32[1,256,128]{2,1,0:T(8,128)S(1)}, f32[1,256,128]{2,1,0:T(8,128)}, u32[]{:S(2)}) copy-start(f32[1,256,128]{2,1,0:T(8,128)} %param.13) | copy-start | bytes 393220
  79.2 17.3 %copy-start.3 = (f32[128,128]{1,0:T(8,128)S(1)}, f32[128,128]{1,0:T(8,128)}, u32[]{:S(2)}) copy-start(f32[128,128]{1,0:T(8,128)} %image_ref.1) | copy-start | bytes 196612
